TPU v7x, 512 devices: a whole 4x8x8 slice. The times are simulated.
512 devices in a mesh: freq: 64 (over y, z_hi, core), chan: 8 (over z_lo, x).
Axes of the slice: x: 4, y: 8, z: 8 (z_hi: 4, z_lo: 2; z = z_hi * 2 + z_lo), core: 2. Of those that a mesh axis runs over, the one named last changes fastest.
Arguments:
- record: bfloat16 [64, 6144, 2048], P('freq', None, 'chan'), may hold values from -12 to 12
Outputs:
- cross: float32 [2, 64, 2048, 1024], P(None, 'freq', 'chan')
All inputs are finite; a program needn't handle non-finite values.
Results may differ from a plain program's by a relative error of at most 0.0032.
Values sent between devices are 32-bit elements; how exact they have to be, the bound alone decides.
No kernel may reach another device: no remote copies, remote signals or barrier semaphores. Data moves between devices by JAX's collectives and lax.ppermute only.
A program may use at most 64 MiB of HBM per device.

v0:
```python
import math

import jax
import jax.numpy as jnp
from jax import lax
from jax.sharding import PartitionSpec as P

NBIN = 64
NEIGH = 40


def shifted(array, axis, by):
    devices = lax.axis_size(axis)
    pairs = [(i, i + by) for i in range(devices) if 0 <= i + by < devices]
    return lax.ppermute(array, axis, pairs)


def dft_table(samples, nbins):
    samples_idx = jnp.arange(samples, dtype=jnp.int32)
    stride = samples // (2 * nbins)
    bin_index = 1 + jnp.arange(nbins, dtype=jnp.int32) * stride
    phase = bin_index[:, None] * samples_idx[None, :] % samples
    angle = 2.0 * math.pi / samples * phase.astype(jnp.float32)
    return jnp.concatenate([jnp.cos(angle), -jnp.sin(angle)], axis=0).astype(jnp.bfloat16)


def neighbour_matrix(nbins):
    rows = jnp.arange(nbins, dtype=jnp.int32)[:, None]
    cols = jnp.arange(nbins, dtype=jnp.int32)[None, :]
    inside = (cols - rows >= -(NEIGH // 2)) & (cols - rows < NEIGH - NEIGH // 2)
    weights = inside.astype(jnp.float32)
    return weights / jnp.sum(weights, axis=1, keepdims=True)


def band_cross(regrouped, widened, band_width):
    highest = lax.Precision.HIGHEST
    windows_all = regrouped.shape[0]
    product_real = jnp.einsum(
        "wbi,wbj->bij", regrouped[:, 0], widened[:, 0], precision=highest
    ) + jnp.einsum("wbi,wbj->bij", regrouped[:, 1], widened[:, 1], precision=highest)
    product_imag = jnp.einsum(
        "wbi,wbj->bij", regrouped[:, 1], widened[:, 0], precision=highest
    ) - jnp.einsum("wbi,wbj->bij", regrouped[:, 0], widened[:, 1], precision=highest)
    stacked = jnp.stack([product_real, product_imag]) / windows_all
    bins_here = stacked.shape[1]
    own_count = stacked.shape[2]
    row_length = stacked.shape[3]
    flattened = stacked.reshape(2, bins_here, own_count * row_length)
    padded_flat = jnp.pad(flattened, ((0, 0), (0, 0), (0, own_count)))
    skewed = padded_flat.reshape(2, bins_here, own_count, row_length + 1)
    return skewed[:, :, :, :band_width]


def shards(record):
    win_dev, samples, ch_dev = record.shape
    table_bins = dft_table(samples, NBIN)
    scaling = 1.0 / math.sqrt(samples)
    spectra = (
        jnp.einsum("ks,wsc->wkc", table_bins, record, preferred_element_type=jnp.float32) * scaling
    )
    spectra = spectra.reshape(win_dev, 2, NBIN, ch_dev)
    power_bins = 0.5 * (spectra[:, 0] * spectra[:, 0] + spectra[:, 1] * spectra[:, 1])
    smooth = jnp.einsum(
        "kj,wjc->wkc", neighbour_matrix(NBIN), power_bins, precision=lax.Precision.HIGHEST
    )
    whitened = spectra * lax.rsqrt(smooth + 1e-06)[:, None]
    regrouped = lax.all_to_all(whitened, "freq", split_axis=2, concat_axis=0, tiled=True)
    reach = lax.axis_size("chan") // 2
    upper_blocks = []
    for offset in range(1, reach + 1):
        upper_blocks.append(shifted(regrouped, "chan", -offset))
    widened = jnp.concatenate([regrouped] + upper_blocks, axis=3)
    return band_cross(regrouped, widened, reach * ch_dev)


def solution(mesh):
    return jax.shard_map(
        shards,
        mesh=mesh,
        in_specs=(P("freq", None, "chan"),),
        out_specs=P(None, "freq", "chan", None),
        check_vma=False,
    )
```

profile of v0, /device:TPU:6, one launch (start us, length us, event | category | flops | bytes accessed | tf_op | source)
XLA Modules:
  0.0 89.6 jit_solution(5236818582385135641)
XLA Ops:
  0.0 0.0 copy-start
  0.0 0.1 convert_reduce_fusion
  0.1 7.2 %cosine_convert_fusion = (bf16[64,6144]{1,0:T(8,128)(2,1)S(1)}, bf16[64,6144]{1,0:T(8,128)(2,1)S(1)}) fusion(s32[64]{0:T(128)S(1)} %multiply_add_fusion), kind=kLoop, calls=%fused_computation.13 | loop fusion | flops 4718592 | bytes 1573120 | tf_op jit(solution)/shard_map/convert
  7.3 0.0 copy-done
  7.3 0.6 fusion.10
  7.9 0.3 fusion.16
  8.2 0.1 copy_multiply_fusion
  8.3 29.8 %all_to_all.18 = f32[1,2,64,256]{3,1,0,2:T(2,128)S(1)} all-to-all(f32[1,2,64,256]{3,1,0,2:T(2,128)S(1)} %copy_multiply_fusion), channel_id=1, replica_groups=mesh['freq'=64,'chan'=8] {'freq'}, dimensions={2} | all-to-all | bytes 262144 | tf_op jit(solution)/shard_map/all_to_all | solution.py:67
  38.2 0.1 fusion.50
  38.3 1.3 %collective-permute-start.3 = (f32[64,2,1,256]{3,1,0,2:T(2,128)S(1)}, f32[64,2,1,256]{3,1,0,2:T(2,128)S(1)}, u32[]{:S(2)}, u32[]{:S(2)}) collective-permute-start(f32[64,2,1,256]{3,1,0,2:T(2,128)S(1)} %bitcast.56), channel_id=1, source_target_pairs={{4,0},{5,1},{6,2},{7,3},{12,8},{13,9},{14,10},{15,11},{20,16},{21,... | collective-permute-start | bytes 393224 | tf_op jit(solution)/shard_map/ppermute | solution.py:15
  39.6 2.4 %collective-permute-start.2 = (f32[64,2,1,256]{3,1,0,2:T(2,128)S(1)}, f32[64,2,1,256]{3,1,0,2:T(2,128)S(1)}, u32[]{:S(2)}, u32[]{:S(2)}) collective-permute-start(f32[64,2,1,256]{3,1,0,2:T(2,128)S(1)} %bitcast.57), channel_id=1, source_target_pairs={{3,0},{4,1},{5,2},{6,3},{7,4},{11,8},{12,9},{13,10},{14,11},{15,12... | collective-permute-start | bytes 393224 | tf_op jit(solution)/shard_map/ppermute | solution.py:15
  42.0 2.2 %collective-permute-start.1 = (f32[64,2,1,256]{3,1,0,2:T(2,128)S(1)}, f32[64,2,1,256]{3,1,0,2:T(2,128)S(1)}, u32[]{:S(2)}, u32[]{:S(2)}) collective-permute-start(f32[64,2,1,256]{3,1,0,2:T(2,128)S(1)} %bitcast.58), channel_id=1, source_target_pairs={{2,0},{3,1},{4,2},{5,3},{6,4},{7,5},{10,8},{11,9},{12,10},{13,11},... | collective-permute-start | bytes 393224 | tf_op jit(solution)/shard_map/ppermute | solution.py:15
  44.2 1.9 %collective-permute-start = (f32[64,2,1,256]{3,1,0,2:T(2,128)S(1)}, f32[64,2,1,256]{3,1,0,2:T(2,128)S(1)}, u32[]{:S(2)}, u32[]{:S(2)}) collective-permute-start(f32[64,2,1,256]{3,1,0,2:T(2,128)S(1)} %bitcast.59), channel_id=1, source_target_pairs={{1,0},{2,1},{3,2},{4,3},{5,4},{6,5},{7,6},{9,8},{10,9},{11,10},{12... | collective-permute-start | bytes 393224 | tf_op jit(solution)/shard_map/ppermute | solution.py:15
  46.2 8.9 %collective-permute-done = f32[64,2,1,256]{3,1,0,2:T(2,128)S(1)} collective-permute-done((f32[64,2,1,256]{3,1,0,2:T(2,128)S(1)}, f32[64,2,1,256]{3,1,0,2:T(2,128)S(1)}, u32[]{:S(2)}, u32[]{:S(2)}) %collective-permute-start) | collective-permute-done | bytes 131104 | tf_op jit(solution)/shard_map/ppermute | solution.py:15
  55.1 0.0 collective-permute-done.1
  55.1 0.0 collective-permute-done.2
  55.2 0.0 collective-permute-done.3
  55.2 0.5 fusion.49
  55.8 1.2 %fusion.17 = f32[256,1280]{1,0:T(8,128)S(1)} fusion(f32[64,1,1,1280]{3,1,0,2:T(1,128)S(1)} %get-tuple-element.6, f32[64,1,1,256]{3,1,0,2:T(1,128)S(1)} %get-tuple-element.8), kind=kOutput, calls=%fused_computation.22 | convolution fusion | flops 251658240 | bytes 1703936 | tf_op jit(solution)/shard_map/wbi,wbj->bij/dot_general | solution.py:43
  57.0 2.3 %fusion.19 = f32[256,1280]{1,0:T(8,128)} fusion(f32[64,1,1,1280]{3,1,0,2:T(1,128)S(1)} %get-tuple-element.6, f32[64,1,1,256]{3,1,0,2:T(1,128)S(1)} %get-tuple-element.7), kind=kOutput, calls=%fused_computation.24 | convolution fusion | flops 251658240 | bytes 1703936 | tf_op jit(solution)/shard_map/wbi,wbj->bij/dot_general | solution.py:40
  59.3 2.3 %convolution_subtract_fusion = f32[256,1280]{1,0:T(8,128)} fusion(f32[256,1280]{1,0:T(8,128)S(1)} %fusion.17, f32[64,1,1,1280]{3,1,0,2:T(1,128)S(1)} %get-tuple-element.5, f32[64,1,1,256]{3,1,0,2:T(1,128)S(1)} %get-tuple-element.7), kind=kOutput, calls=%fused_computation.2 | convolution fusion | flops 251985920 | bytes 3014656 | tf_op jit(solution)/shard_map/wbi,wbj->bij/dot_general | solution.py:41
  61.6 3.7 %stack.10 = f32[1,1,327680]{2,1,0:T(1,128)} reshape(f32[256,1280]{1,0:T(8,128)} %convolution_subtract_fusion) | data formatting | bytes 2621440 | tf_op jit(solution)/shard_map/stack | solution.py:44
  65.3 3.6 %convolution_add_fusion = f32[256,1280]{1,0:T(8,128)} fusion(f32[256,1280]{1,0:T(8,128)} %fusion.19, f32[64,1,1,1280]{3,1,0,2:T(1,128)S(1)} %get-tuple-element.5, f32[64,1,1,256]{3,1,0,2:T(1,128)S(1)} %get-tuple-element.8), kind=kOutput, calls=%fused_computation.3 | convolution fusion | flops 251985920 | bytes 3014656 | tf_op jit(solution)/shard_map/wbi,wbj->bij/dot_general | solution.py:38
  68.9 3.7 %stack.9 = f32[1,1,327680]{2,1,0:T(1,128)} reshape(f32[256,1280]{1,0:T(8,128)} %convolution_add_fusion) | data formatting | bytes 2621440 | tf_op jit(solution)/shard_map/stack | solution.py:44
  72.7 4.1 %maximum_multiply_fusion = f32[2,1,327680]{2,0,1:T(2,128)S(1)} fusion(f32[1,1,327680]{2,0,1:T(1,128)} %bitcast.53, f32[1,1,327680]{2,0,1:T(1,128)} %bitcast.54), kind=kLoop, calls=%fused_computation.4 | loop fusion | flops 1310720 | bytes 5242880 | tf_op jit(solution)/shard_map/div | solution.py:44
  76.8 2.5 %pad.4 = f32[2,1,327936]{2,0,1:T(2,128)} pad(f32[2,1,327680]{2,0,1:T(2,128)S(1)} %maximum_multiply_fusion, f32[]{:T(128)} %constant.32.clone.1), padding=0_0x0_0x0_256 | pad | bytes 5244932 | tf_op jit(solution)/shard_map/jit(_pad)/pad | solution.py:49
  79.2 7.2 %reshape.132 = f32[2,1,256,1281]{3,2,0,1:T(8,128)} reshape(f32[2,1,327936]{2,0,1:T(2,128)} %pad.4) | data formatting | bytes 5246976 | tf_op jit(solution)/shard_map/reshape | solution.py:50
  86.4 3.2 %slice_bitcast_fusion = f32[2,1,256,1024]{3,2,1,0:T(8,128)} fusion(f32[2,1,256,1281]{3,2,0,1:T(8,128)} %reshape.132), kind=kLoop, calls=%fused_computation.6 | loop fusion | bytes 4194304 | tf_op jit(solution)/shard_map/slice | solution.py:51
  (6 shorter events, 0.2 us)
Async XLA Ops:
  0.0 7.3 %copy-start = (bf16[1,6144,256]{2,1,0:T(8,128)(2,1)S(1)}, bf16[1,6144,256]{2,1,0:T(8,128)(2,1)}, u32[]{:S(2)}) copy-start(bf16[1,6144,256]{2,1,0:T(8,128)(2,1)} %param.1) | copy-start | bytes 9437188
  38.3 16.9 %collective-permute-start.3 = (f32[64,2,1,256]{3,1,0,2:T(2,128)S(1)}, f32[64,2,1,256]{3,1,0,2:T(2,128)S(1)}, u32[]{:S(2)}, u32[]{:S(2)}) collective-permute-start(f32[64,2,1,256]{3,1,0,2:T(2,128)S(1)} %bitcast.56), channel_id=1, source_target_pairs={{4,0},{5,1},{6,2},{7,3},{12,8},{13,9},{14,10},{15,11},{20,16},{21,... | collective-permute-start | bytes 393224 | tf_op jit(solution)/shard_map/ppermute | solution.py:15
  39.6 15.6 %collective-permute-start.2 = (f32[64,2,1,256]{3,1,0,2:T(2,128)S(1)}, f32[64,2,1,256]{3,1,0,2:T(2,128)S(1)}, u32[]{:S(2)}, u32[]{:S(2)}) collective-permute-start(f32[64,2,1,256]{3,1,0,2:T(2,128)S(1)} %bitcast.57), channel_id=1, source_target_pairs={{3,0},{4,1},{5,2},{6,3},{7,4},{11,8},{12,9},{13,10},{14,11},{15,12... | collective-permute-start | bytes 393224 | tf_op jit(solution)/shard_map/ppermute | solution.py:15
  42.0 13.1 %collective-permute-start.1 = (f32[64,2,1,256]{3,1,0,2:T(2,128)S(1)}, f32[64,2,1,256]{3,1,0,2:T(2,128)S(1)}, u32[]{:S(2)}, u32[]{:S(2)}) collective-permute-start(f32[64,2,1,256]{3,1,0,2:T(2,128)S(1)} %bitcast.58), channel_id=1, source_target_pairs={{2,0},{3,1},{4,2},{5,3},{6,4},{7,5},{10,8},{11,9},{12,10},{13,11},... | collective-permute-start | bytes 393224 | tf_op jit(solution)/shard_map/ppermute | solution.py:15
  44.2 10.9 %collective-permute-start = (f32[64,2,1,256]{3,1,0,2:T(2,128)S(1)}, f32[64,2,1,256]{3,1,0,2:T(2,128)S(1)}, u32[]{:S(2)}, u32[]{:S(2)}) collective-permute-start(f32[64,2,1,256]{3,1,0,2:T(2,128)S(1)} %bitcast.59), channel_id=1, source_target_pairs={{1,0},{2,1},{3,2},{4,3},{5,4},{6,5},{7,6},{9,8},{10,9},{11,10},{12... | collective-permute-start | bytes 393224 | tf_op jit(solution)/shard_map/ppermute | solution.py:15
where the time goes:
time: 90 us; the launch traced here: 89.6 us
  blocking collectives  29.8 us (33%)
  local copies, waits for them, and re-layouts  21 us (23%)
  other arithmetic  11.5 us (13%)
  matrix products  10.3 us (11%)
  waiting for transfers between devices  8.91 us (10%)
  starting transfers between devices  7.82 us (9%)
    all_to_all x1, blocking collectives, shards(): lax.all_to_all(whitened, 'freq', split_axis=2, concat_axis=0, tiled=True)  29.8 us
    ppermute x4, waiting for transfers between devices, shifted(): return lax.ppermute(array, axis, pairs)  8.91 us
    ppermute x4, starting transfers between devices, shifted(): return lax.ppermute(array, axis, pairs)  7.82 us
    another operation x2, local copies, waits for them, and re-layouts, band_cross(): stacked = jnp.stack([product_real, product_imag]) / windows_all  7.43 us
    reshape x1, local copies, waits for them, and re-layouts, band_cross(): skewed = padded_flat.reshape(2, bins_here, own_count, row_length + 1)  7.19 us
    another operation x1, other arithmetic  7.17 us
    div x1, other arithmetic, band_cross(): stacked = jnp.stack([product_real, product_imag]) / windows_all  4.12 us
    dot_general x1, matrix products, band_cross(): jnp.einsum('wbi,wbj->bij', regrouped[:, 0], widened[:, 0], precision=high...  3.61 us
  transfers between devices with their start and end apart: 4, of which 1 were waited for; matrix products, arithmetic and copies ran while one was open for 0% of the time, Pallas kernels for 0%

commit v1 on v0

v1 whole, which is shorter than its diff:
```python
import functools
import math

import jax
import jax.numpy as jnp
from jax import lax
from jax.experimental import pallas as pl
from jax.experimental.pallas import tpu as pltpu
from jax.sharding import PartitionSpec as P

NBIN = 64
NEIGH = 40
CHUNKS = 6
ROWS = 64
LANES = 128
WIDE = 256


def neighbour_weights():
    row = lax.broadcasted_iota(jnp.int32, (NBIN, NBIN), 0)
    col = lax.broadcasted_iota(jnp.int32, (NBIN, NBIN), 1)
    below, above = NEIGH // 2, NEIGH - NEIGH // 2
    inside = (col - row >= -below) & (col - row < above)
    count = jnp.minimum(row + above, NBIN) - jnp.maximum(row - below, 0)
    return jnp.where(inside, 1.0 / count.astype(jnp.float32), 0.0)


def base_angles(samples):
    stride, period = samples // (2 * NBIN), 2 * NBIN
    k = lax.broadcasted_iota(jnp.int32, (NBIN, period), 0)
    s = lax.broadcasted_iota(jnp.int32, (NBIN, period), 1)
    phase = s + stride * ((k * s) & (period - 1))
    return 2.0 * math.pi / samples * phase.astype(jnp.float32)


def whiten_kernel(samples, record_ref, out_ref, buf_ref, table_ref, sems):
    chunk = samples // CHUNKS
    period = 2 * NBIN
    turns = samples // period

    def fetch(n):
        part = pl.ds(n * chunk, chunk)
        return pltpu.make_async_copy(record_ref.at[0, part], buf_ref.at[part], sems.at[n])

    for n in range(CHUNKS):
        fetch(n).start()
    angle = base_angles(samples)
    cos, sin = jnp.cos(angle), jnp.sin(angle)
    for m in range(turns):
        c, s = math.cos(2.0 * math.pi * m / turns), math.sin(2.0 * math.pi * m / turns)
        part = pl.ds(m * period, period)
        table_ref[:NBIN, part] = (c * cos - s * sin).astype(jnp.bfloat16)
        table_ref[NBIN:, part] = (-(s * cos + c * sin)).astype(jnp.bfloat16)
    total = None
    for n in range(CHUNKS):
        fetch(n).wait()
        part = pl.ds(n * chunk, chunk)
        term = jnp.dot(table_ref[:, part], buf_ref[part], preferred_element_type=jnp.float32)
        total = term if total is None else total + term
    scaling = 1.0 / math.sqrt(samples)
    re, im = total[:NBIN] * scaling, total[NBIN:] * scaling
    power = 0.5 * (re * re + im * im)
    smooth = jnp.dot(neighbour_weights(), power, precision=lax.Precision.HIGHEST,
                     preferred_element_type=jnp.float32)
    gain = lax.rsqrt(smooth + 1e-06)
    half = re.shape[1] // LANES
    for n in range(half):
        part = slice(n * LANES, (n + 1) * LANES)
        out_ref[:, n, :] = (re * gain)[:, part]
        out_ref[:, half + n, :] = (im * gain)[:, part]


def whitened_bins(record):
    _, samples, ch = record.shape
    return pl.pallas_call(
        functools.partial(whiten_kernel, samples),
        in_specs=[pl.BlockSpec(memory_space=pltpu.HBM)],
        out_specs=pl.BlockSpec(memory_space=pltpu.VMEM),
        out_shape=jax.ShapeDtypeStruct((NBIN, 2 * ch // LANES, LANES), jnp.float32),
        scratch_shapes=[
            pltpu.VMEM((samples, ch), jnp.bfloat16),
            pltpu.VMEM((2 * NBIN, samples), jnp.bfloat16),
            pltpu.SemaphoreType.DMA((CHUNKS,)),
        ],
        compiler_params=pltpu.CompilerParams(vmem_limit_bytes=52 * 1024 * 1024),
        name="whiten",
    )(record)


def split_terms(x):
    high = x.astype(jnp.bfloat16)
    return high, (x - high.astype(jnp.float32)).astype(jnp.bfloat16)


def real_imag(block_ref):
    half = block_ref.shape[1] // 2
    tiles = [block_ref[:, n, :] for n in range(2 * half)]
    return jnp.concatenate(tiles[:half], axis=1), jnp.concatenate(tiles[half:], axis=1)


def left_kernel(own_ref, left_ref):
    re, im = real_imag(own_ref)
    scale = 1.0 / own_ref.shape[0]
    re, im = (re * scale).T, (im * scale).T
    left = jnp.concatenate(
        [jnp.concatenate([re, im], axis=1), jnp.concatenate([im, -re], axis=1)], axis=0
    )
    high, low = split_terms(left)
    left_ref[...] = jnp.concatenate([high, low, high], axis=1)


def left_terms(own):
    windows, pieces, lanes = own.shape
    return pl.pallas_call(
        left_kernel,
        in_specs=[pl.BlockSpec(memory_space=pltpu.VMEM)],
        out_specs=pl.BlockSpec(memory_space=pltpu.VMEM),
        out_shape=jax.ShapeDtypeStruct((pieces * lanes, 6 * windows), jnp.bfloat16),
        compiler_params=pltpu.CompilerParams(vmem_limit_bytes=16 * 1024 * 1024),
        cost_estimate=pl.CostEstimate(flops=0, bytes_accessed=1 << 20, transcendentals=0),
        name="left",
    )(own)


def region_kernel(first, count, fresh, left_ref, *refs):
    blocks = refs[:count + 1]
    out_ref, wide_ref, prod_ref, band_ref, sems = refs[count + 1 if fresh else count + 2:]
    ch = wide_ref.shape[1]
    tiles = ch // LANES
    row = lax.broadcasted_iota(jnp.int32, (ROWS, LANES), 0)
    lane = lax.broadcasted_iota(jnp.int32, (ROWS, LANES), 1)
    copies = []
    for n in range(count + 1):
        re, im = real_imag(blocks[n])
        high, low = split_terms(jnp.concatenate([re, im], axis=0))
        wide_ref[...] = jnp.concatenate([high, high, low], axis=0)
        prod_ref[:, n * ch:(n + 1) * ch] = jnp.dot(
            left_ref[...], wide_ref[...], preferred_element_type=jnp.float32
        )
        if n == 0:
            continue
        here = pl.ds((n - 1) * ch, ch)
        there = pl.ds((first + n - 1) * ch, ch)
        for part in range(2):
            for start in range(0, ch, ROWS):
                low_rows = start % LANES
                head = (start // LANES) + (n - 1) * tiles
                source = (lane + row + low_rows) % LANES
                keep = lane < LANES - low_rows - row
                rows = pl.ds(part * ch + start, ROWS)

                def turned(v):
                    tile = prod_ref[rows, pl.ds((head + v) * LANES, LANES)]
                    return jnp.take_along_axis(tile, source, axis=1, mode="promise_in_bounds")

                before = turned(0)
                for v in range(tiles):
                    after = turned(v + 1)
                    band_ref[part, pl.ds(start, ROWS), pl.ds((n - 1) * ch + v * LANES, LANES)] = (
                        jnp.where(keep, before, after)
                    )
                    before = after
            copy = pltpu.make_async_copy(
                band_ref.at[part, :, here], out_ref.at[part, 0, :, there], sems.at[n - 1, part]
            )
            copy.start()
            copies.append(copy)
    for copy in copies:
        copy.wait()


def region(left, blocks, first, band, out=None):
    windows, pieces, lanes = blocks[0].shape
    ch = pieces * lanes // 2
    count = len(blocks) - 1
    vmem = pl.BlockSpec(memory_space=pltpu.VMEM)
    hbm = pl.BlockSpec(memory_space=pltpu.HBM)
    fresh = out is None
    return pl.pallas_call(
        functools.partial(region_kernel, first, count, fresh),
        in_specs=[vmem] * (count + 2) + ([] if fresh else [hbm]),
        out_specs=hbm,
        out_shape=jax.ShapeDtypeStruct((2, 1, ch, band), jnp.float32),
        scratch_shapes=[
            pltpu.VMEM((6 * windows, ch), jnp.bfloat16),
            pltpu.VMEM((2 * ch, (count + 1) * ch), jnp.float32),
            pltpu.VMEM((2, ch, count * ch), jnp.float32),
            pltpu.SemaphoreType.DMA((count, 2)),
        ],
        input_output_aliases={} if fresh else {count + 2: 0},
        compiler_params=pltpu.CompilerParams(vmem_limit_bytes=32 * 1024 * 1024),
        cost_estimate=pl.CostEstimate(flops=0, bytes_accessed=3 << 20, transcendentals=0),
        name="region",
    )(left, *blocks, *([] if fresh else [out]))


def cross_all(blocks):
    _, pieces, lanes = blocks[0].shape
    reach = len(blocks) - 1
    left = left_terms(blocks[0])
    band = reach * pieces * lanes // 2
    out = region(left, blocks[3:5], 3, band)
    out = region(left, blocks[0:2], 0, band, out)
    return region(left, blocks[1:4], 1, band, out)


def upper_blocks(own):
    count = lax.axis_size("chan")
    half = count // 2

    def moved(array, pairs):
        return lax.ppermute(array, "chan", pairs)

    fourth = moved(own, [(c, c - half) for c in range(half, count)])
    third = moved(own, [(c, c - 3) for c in range(3, count)])
    first = moved(own, [(c, c - 1) for c in range(1, count)])
    handed = jnp.where(lax.axis_index("chan") < 2, fourth, own)
    second = moved(
        handed,
        [(c, c - 2) for c in range(2, count) if c // half == (c - 2) // half]
        + [(c, c + 2) for c in range(2)],
    )
    return [first, second, third, fourth]


def shards(record):
    bins = whitened_bins(record)
    own = lax.all_to_all(bins, "freq", split_axis=0, concat_axis=0, tiled=True)
    return cross_all([own] + upper_blocks(own))


def solution(mesh):
    return jax.shard_map(
        shards,
        mesh=mesh,
        in_specs=(P("freq", None, "chan"),),
        out_specs=P(None, "freq", "chan", None),
        check_vma=False,
    )
```

time: 90 us -> 51.6 us (0.57)
  the two profiles are of different devices: /device:TPU:6 before, /device:TPU:4 now
where the time goes in v1:
time: 51.6 us; the launch traced here: 51.3 us
  blocking collectives  29.8 us (58%)
  Pallas kernels  8.38 us (16%)
  starting transfers between devices  7.13 us (14%)
  waiting for transfers between devices  5.89 us (11%)
    all_to_all x1, blocking collectives, shards(): own = lax.all_to_all(bins, 'freq', split_axis=0, concat_axis=0, tiled=True)  29.8 us
    ppermute x4, starting transfers between devices, moved(): return lax.ppermute(array, 'chan', pairs)  7.13 us
    ppermute x4, waiting for transfers between devices, moved(): return lax.ppermute(array, 'chan', pairs)  5.89 us
    pallas_call x3, Pallas kernels, region(): pl.pallas_call(functools.partial(region_kernel, first, count, fresh), in_...  5.42 us
    pallas_call x1, Pallas kernels, whitened_bins(): pl.pallas_call(functools.partial(whiten_kernel, samples), in_specs=[pl.Bl...  2.7 us
  transfers between devices with their start and end apart: 4, of which 2 were waited for; matrix products, arithmetic and copies ran while one was open for 0% of the time, Pallas kernels for 7%

profile of v1, /device:TPU:4, one launch (start us, length us, event | category | flops | bytes accessed | tf_op | source)
XLA Modules:
  0.0 51.3 jit_solution(6098361316576982383)
XLA Ops:
  0.0 2.7 %whiten.1 = f32[64,4,128]{2,1,0:T(4,128)S(1)} custom-call(bf16[1,6144,256]{2,1,0:T(8,128)(2,1)} %record_ref.1), custom_call_target="tpu_custom_call" | custom-call | tf_op jit(solution)/shard_map/whiten/pallas_call | solution.py:75
  2.7 29.8 %all_to_all.5.own_ref.refs_0_ = f32[64,4,128]{2,1,0:T(4,128)S(1)} all-to-all(f32[64,4,128]{2,1,0:T(4,128)S(1)} %whiten.1), channel_id=1, replica_groups=mesh['freq'=64,'chan'=8] {'freq'}, dimensions={0} | all-to-all | bytes 262144 | tf_op jit(solution)/shard_map/all_to_all | solution.py:228
  32.5 1.3 %collective-permute-start.1 = (f32[64,4,128]{2,1,0:T(4,128)S(1)}, f32[64,4,128]{2,1,0:T(4,128)S(1)}, u32[]{:S(2)}, u32[]{:S(2)}) collective-permute-start(f32[64,4,128]{2,1,0:T(4,128)S(1)} %all_to_all.5.own_ref.refs_0_), channel_id=1, source_target_pairs={{4,0},{5,1},{6,2},{7,3},{12,8},{13,9},{14,10},{15,11},{20,16},{21,... | collective-permute-start | bytes 393224 | tf_op jit(solution)/shard_map/ppermute | solution.py:212
  33.8 1.3 %collective-permute-start.3 = (f32[64,4,128]{2,1,0:T(4,128)S(1)}, f32[64,4,128]{2,1,0:T(4,128)S(1)}, u32[]{:S(2)}, u32[]{:S(2)}) collective-permute-start(f32[64,4,128]{2,1,0:T(4,128)S(1)} %all_to_all.5.own_ref.refs_0_), channel_id=1, source_target_pairs={{3,0},{4,1},{5,2},{6,3},{7,4},{11,8},{12,9},{13,10},{14,11},{15,12... | collective-permute-start | bytes 393224 | tf_op jit(solution)/shard_map/ppermute | solution.py:212
  35.1 2.4 %collective-permute-start = (f32[64,4,128]{2,1,0:T(4,128)S(1)}, f32[64,4,128]{2,1,0:T(4,128)S(1)}, u32[]{:S(2)}, u32[]{:S(2)}) collective-permute-start(f32[64,4,128]{2,1,0:T(4,128)S(1)} %all_to_all.5.own_ref.refs_0_), channel_id=1, source_target_pairs={{1,0},{2,1},{3,2},{4,3},{5,4},{6,5},{7,6},{9,8},{10,9},{11,10},{12... | collective-permute-start | bytes 393224 | tf_op jit(solution)/shard_map/ppermute | solution.py:212
  37.6 3.2 %collective-permute-done.1.refs_1_ = f32[64,4,128]{2,1,0:T(4,128)S(1)} collective-permute-done((f32[64,4,128]{2,1,0:T(4,128)S(1)}, f32[64,4,128]{2,1,0:T(4,128)S(1)}, u32[]{:S(2)}, u32[]{:S(2)}) %collective-permute-start.1) | collective-permute-done | bytes 131104 | tf_op jit(solution)/shard_map/ppermute | solution.py:212
  40.8 2.1 %collective-permute-start.2 = (f32[64,4,128]{2,1,0:T(4,128)S(1)}, f32[64,4,128]{2,1,0:T(4,128)S(1)}, u32[]{:S(2)}, u32[]{:S(2)}) collective-permute-start(f32[64,4,128]{2,1,0:T(4,128)S(1)} %bitcast.5), channel_id=1, source_target_pairs={{2,0},{3,1},{6,4},{7,5},{0,2},{1,3},{10,8},{11,9},{14,12},{15,13},... | collective-permute-start | bytes 393224 | tf_op jit(solution)/shard_map/ppermute | solution.py:212
  42.9 0.3 left.1.left_ref
  43.2 0.0 collective-permute-done.3.refs_0_.refs_2_
  43.2 1.6 %region.3.refs_2_ = f32[2,1,256,1024]{3,2,1,0:T(8,128)} custom-call(bf16[512,384]{1,0:T(8,128)(2,1)S(1)} %left.1.left_ref, f32[64,4,128]{2,1,0:T(4,128)S(1)} %collective-permute-done.3.refs_0_.refs_2_, f32[64,4,128]{2,1,0:T(4,128)S(1)} %collective-permute-done.1.refs_1_), custom_call_target="tpu_custom_call" | custom-call | bytes 3145728 | tf_op jit(solution)/shard_map/region/pallas_call | solution.py:179
  44.8 0.0 collective-permute-done.refs_1_.refs_0_
  44.8 1.6 %region.4.refs_3_ = f32[2,1,256,1024]{3,2,1,0:T(8,128)} custom-call(bf16[512,384]{1,0:T(8,128)(2,1)S(1)} %left.1.left_ref, f32[64,4,128]{2,1,0:T(4,128)S(1)} %all_to_all.5.own_ref.refs_0_, f32[64,4,128]{2,1,0:T(4,128)S(1)} %collective-permute-done.refs_1_.refs_0_, f32[2,1,256,1024]{3,2,1,0:T(8,128)} %region.3.refs_2_), custom_call_target="tpu_custom_call", output_to_operand_aliasing={{}: (3, {})} | custom-call | bytes 3145728 | tf_op jit(solution)/shard_map/region/pallas_call | solution.py:179
  46.5 2.7 %collective-permute-done.2.refs_1_ = f32[64,4,128]{2,1,0:T(4,128)S(1)} collective-permute-done((f32[64,4,128]{2,1,0:T(4,128)S(1)}, f32[64,4,128]{2,1,0:T(4,128)S(1)}, u32[]{:S(2)}, u32[]{:S(2)}) %collective-permute-start.2) | collective-permute-done | bytes 131104 | tf_op jit(solution)/shard_map/ppermute | solution.py:212
  49.2 2.2 %region.5 = f32[2,1,256,1024]{3,2,1,0:T(8,128)} custom-call(bf16[512,384]{1,0:T(8,128)(2,1)S(1)} %left.1.left_ref, f32[64,4,128]{2,1,0:T(4,128)S(1)} %collective-permute-done.refs_1_.refs_0_, f32[64,4,128]{2,1,0:T(4,128)S(1)} %collective-permute-done.2.refs_1_, ...), custom_call_target="tpu_custom_call", output_to_operand_aliasing={{}: (4, {})} | custom-call | bytes 3145728 | tf_op jit(solution)/shard_map/region/pallas_call | solution.py:179
  (1 shorter events, 0.0 us)
Async XLA Ops:
  32.5 8.2 %collective-permute-start.1 = (f32[64,4,128]{2,1,0:T(4,128)S(1)}, f32[64,4,128]{2,1,0:T(4,128)S(1)}, u32[]{:S(2)}, u32[]{:S(2)}) collective-permute-start(f32[64,4,128]{2,1,0:T(4,128)S(1)} %all_to_all.5.own_ref.refs_0_), channel_id=1, source_target_pairs={{4,0},{5,1},{6,2},{7,3},{12,8},{13,9},{14,10},{15,11},{20,16},{21,... | collective-permute-start | bytes 393224 | tf_op jit(solution)/shard_map/ppermute | solution.py:212
  33.8 9.3 %collective-permute-start.3 = (f32[64,4,128]{2,1,0:T(4,128)S(1)}, f32[64,4,128]{2,1,0:T(4,128)S(1)}, u32[]{:S(2)}, u32[]{:S(2)}) collective-permute-start(f32[64,4,128]{2,1,0:T(4,128)S(1)} %all_to_all.5.own_ref.refs_0_), channel_id=1, source_target_pairs={{3,0},{4,1},{5,2},{6,3},{7,4},{11,8},{12,9},{13,10},{14,11},{15,12... | collective-permute-start | bytes 393224 | tf_op jit(solution)/shard_map/ppermute | solution.py:212
  35.1 9.7 %collective-permute-start = (f32[64,4,128]{2,1,0:T(4,128)S(1)}, f32[64,4,128]{2,1,0:T(4,128)S(1)}, u32[]{:S(2)}, u32[]{:S(2)}) collective-permute-start(f32[64,4,128]{2,1,0:T(4,128)S(1)} %all_to_all.5.own_ref.refs_0_), channel_id=1, source_target_pairs={{1,0},{2,1},{3,2},{4,3},{5,4},{6,5},{7,6},{9,8},{10,9},{11,10},{12... | collective-permute-start | bytes 393224 | tf_op jit(solution)/shard_map/ppermute | solution.py:212
  40.8 8.4 %collective-permute-start.2 = (f32[64,4,128]{2,1,0:T(4,128)S(1)}, f32[64,4,128]{2,1,0:T(4,128)S(1)}, u32[]{:S(2)}, u32[]{:S(2)}) collective-permute-start(f32[64,4,128]{2,1,0:T(4,128)S(1)} %bitcast.5), channel_id=1, source_target_pairs={{2,0},{3,1},{6,4},{7,5},{0,2},{1,3},{10,8},{11,9},{14,12},{15,13},... | collective-permute-start | bytes 393224 | tf_op jit(solution)/shard_map/ppermute | solution.py:212

commit v2 on v1

v2 whole, which is shorter than its diff:
```python
import functools
import math

import jax
import jax.numpy as jnp
from jax import lax
from jax.experimental import pallas as pl
from jax.experimental.pallas import tpu as pltpu
from jax.sharding import Mesh, PartitionSpec as P

NBIN = 64
NEIGH = 40
CHUNKS = 4
ROWS = 64
LANES = 128


def bin_of(row):
    return 2 * (row & (NBIN // 2 - 1)) + row // (NBIN // 2)


def neighbour_weights():
    row = bin_of(lax.broadcasted_iota(jnp.int32, (NBIN, NBIN), 0))
    col = bin_of(lax.broadcasted_iota(jnp.int32, (NBIN, NBIN), 1))
    below, above = NEIGH // 2, NEIGH - NEIGH // 2
    inside = (col - row >= -below) & (col - row < above)
    count = jnp.minimum(row + above, NBIN) - jnp.maximum(row - below, 0)
    return jnp.where(inside, 1.0 / count.astype(jnp.float32), 0.0)


def base_angles(samples):
    stride, period = samples // (2 * NBIN), 2 * NBIN
    k = bin_of(lax.broadcasted_iota(jnp.int32, (NBIN, period), 0))
    s = lax.broadcasted_iota(jnp.int32, (NBIN, period), 1)
    phase = s + stride * ((k * s) & (period - 1))
    return 2.0 * math.pi / samples * phase.astype(jnp.float32)


def whiten_kernel(samples, core_ref, record_ref, keep_ref, send_ref, buf_ref, table_ref, sems):
    chunk = samples // CHUNKS
    quarter = samples // 4
    period = 2 * NBIN
    turns = samples // period

    def fetch(n):
        part = pl.ds(n * chunk, chunk)
        return pltpu.make_async_copy(record_ref.at[0, part], buf_ref.at[part], sems.at[n])

    for n in range(CHUNKS):
        fetch(n).start(priority=n % 2)
    angle = base_angles(samples)
    cos, sin = jnp.cos(angle), jnp.sin(angle)
    for m in range(quarter // period):
        c, s = math.cos(2.0 * math.pi * m / turns), math.sin(2.0 * math.pi * m / turns)
        part = pl.ds(m * period, period)
        table_ref[:NBIN, part] = (c * cos - s * sin).astype(jnp.bfloat16)
        table_ref[NBIN:, part] = (-s * cos - c * sin).astype(jnp.bfloat16)
    sums = [None] * 4
    for n in range(CHUNKS):
        fetch(n).wait()
        q, start = divmod(n * chunk, quarter)
        term = jnp.dot(table_ref[:, pl.ds(start, chunk)], buf_ref[pl.ds(n * chunk, chunk)],
                       preferred_element_type=jnp.float32)
        sums[q] = term if sums[q] is None else sums[q] + term
    even, odd = sums[0] - sums[2], sums[1] - sums[3]
    scaling = 1.0 / math.sqrt(samples)
    re = (even[:NBIN] + odd[NBIN:]) * scaling
    im = (even[NBIN:] - odd[:NBIN]) * scaling
    power = 0.5 * (re * re + im * im)
    smooth = jnp.dot(neighbour_weights(), power, precision=lax.Precision.HIGHEST,
                     preferred_element_type=jnp.float32)
    gain = lax.rsqrt(smooth + 1e-06)
    re, im = re * gain, im * gain
    even_core = core_ref[0] == 0
    pieces = re.shape[1] // LANES
    for p, value in enumerate((re, im)):
        lower, upper = value[:NBIN // 2], value[NBIN // 2:]
        keep, send = jnp.where(even_core, lower, upper), jnp.where(even_core, upper, lower)
        for n in range(pieces):
            part = slice(n * LANES, (n + 1) * LANES)
            keep_ref[:, p * pieces + n, :] = keep[:, part]
            send_ref[:, p * pieces + n, :] = send[:, part]


def whitened_bins(core, record):
    _, samples, ch = record.shape
    vmem = pl.BlockSpec(memory_space=pltpu.VMEM)
    shape = jax.ShapeDtypeStruct((NBIN // 2, 2 * ch // LANES, LANES), jnp.float32)
    return pl.pallas_call(
        functools.partial(whiten_kernel, samples),
        in_specs=[
            pl.BlockSpec(memory_space=pltpu.SMEM),
            pl.BlockSpec(memory_space=pltpu.HBM),
        ],
        out_specs=(vmem, vmem),
        out_shape=(shape, shape),
        scratch_shapes=[
            pltpu.VMEM((samples, ch), jnp.bfloat16),
            pltpu.VMEM((2 * NBIN, samples // 4), jnp.bfloat16),
            pltpu.SemaphoreType.DMA((CHUNKS,)),
        ],
        compiler_params=pltpu.CompilerParams(vmem_limit_bytes=52 * 1024 * 1024),
        name="whiten",
    )(core, record)


def split_terms(x):
    high = x.astype(jnp.bfloat16)
    return high, (x - high.astype(jnp.float32)).astype(jnp.bfloat16)


def real_imag(block_ref):
    half = block_ref.shape[1] // 2
    tiles = [block_ref[:, n, :] for n in range(2 * half)]
    return jnp.concatenate(tiles[:half], axis=1), jnp.concatenate(tiles[half:], axis=1)


def product(left_ref, block_ref, wide_ref, out_ref):
    re, im = real_imag(block_ref)
    high, low = split_terms(jnp.concatenate([re, im], axis=0))
    wide_ref[...] = jnp.concatenate([high, high, low], axis=0)
    halves, parts, rows, ch = out_ref.shape
    for a in range(halves):
        here = pl.ds(a * parts * rows, parts * rows)
        out_ref[a] = jnp.dot(
            left_ref[here], wide_ref[...], preferred_element_type=jnp.float32
        ).reshape(parts, rows, ch)


def own_kernel(own_ref, left_ref, prod_ref, wide_ref):
    re, im = real_imag(own_ref)
    scale = 1.0 / own_ref.shape[0]
    re, im = (re * scale).T, (im * scale).T
    rows = re.shape[0] // 2
    for a in range(2):
        r, i = re[a * rows:(a + 1) * rows], im[a * rows:(a + 1) * rows]
        left = jnp.concatenate(
            [jnp.concatenate([r, i], axis=1), jnp.concatenate([i, -r], axis=1)], axis=0
        )
        high, low = split_terms(left)
        left_ref[2 * a * rows:2 * (a + 1) * rows] = jnp.concatenate([high, low, high], axis=1)
    product(left_ref, own_ref, wide_ref, prod_ref)


def product_shape(ch):
    return jax.ShapeDtypeStruct((2, 2, ch // 2, ch), jnp.float32)


def own_terms(own):
    windows, pieces, lanes = own.shape
    ch = pieces * lanes // 2
    vmem = pl.BlockSpec(memory_space=pltpu.VMEM)
    return pl.pallas_call(
        own_kernel,
        in_specs=[vmem],
        out_specs=(vmem, vmem),
        out_shape=(
            jax.ShapeDtypeStruct((2 * ch, 6 * windows), jnp.bfloat16),
            product_shape(ch),
        ),
        scratch_shapes=[pltpu.VMEM((6 * windows, ch), jnp.bfloat16)],
        compiler_params=pltpu.CompilerParams(vmem_limit_bytes=16 * 1024 * 1024),
        cost_estimate=pl.CostEstimate(flops=0, bytes_accessed=1 << 20, transcendentals=0),
        name="own",
    )(own)


def region_kernel(first, given, keep, fresh, left_ref, *refs):
    count = len(given)
    blocks, refs = refs[:count], refs[count if fresh else count + 1:]
    out_ref, kept, refs = refs[0], refs[1:1 + len(keep)], refs[1 + len(keep):]
    wide_ref, prod_ref, band_ref, sems = refs
    products = []
    for n in range(count):
        if given[n]:
            products.append(blocks[n])
            continue
        target = kept[keep.index(n)] if n in keep else prod_ref.at[n]
        product(left_ref, blocks[n], wide_ref, target)
        products.append(target)
    ch = wide_ref.shape[1]
    rows = ch // 2
    tiles = ch // LANES
    row = lax.broadcasted_iota(jnp.int32, (ROWS, LANES), 0)
    lane = lax.broadcasted_iota(jnp.int32, (ROWS, LANES), 1)
    copies = []
    for a in range(2):
        for part in range(2):
            for start in range(0, rows, ROWS):
                source = (lane + row + start) % LANES
                stays = lane < LANES - start - row

                def turned(tile):
                    n, lanes = divmod(tile, tiles)
                    value = products[n][a, part, pl.ds(start, ROWS), pl.ds(lanes * LANES, LANES)]
                    return jnp.take_along_axis(value, source, axis=1, mode="promise_in_bounds")

                before = turned(a)
                for v in range((count - 1) * tiles):
                    after = turned(a + v + 1)
                    band_ref[part, pl.ds(a * rows + start, ROWS), pl.ds(v * LANES, LANES)] = (
                        jnp.where(stays, before, after)
                    )
                    before = after
            here = pl.ds(a * rows, rows)
            there = pl.ds(first * ch, (count - 1) * ch)
            copy = pltpu.make_async_copy(
                band_ref.at[part, here], out_ref.at[part, 0, here, there], sems.at[a, part]
            )
            copy.start()
            copies.append(copy)
    for copy in copies:
        copy.wait()


def region(left, blocks, first, band, out=None, keep=()):
    ch = left.shape[0] // 2
    depth = left.shape[1]
    count = len(blocks)
    vmem = pl.BlockSpec(memory_space=pltpu.VMEM)
    hbm = pl.BlockSpec(memory_space=pltpu.HBM)
    fresh = out is None
    given = tuple(block.ndim == 4 for block in blocks)
    return pl.pallas_call(
        functools.partial(region_kernel, first, given, keep, fresh),
        in_specs=[vmem] * (count + 1) + ([] if fresh else [hbm]),
        out_specs=(hbm,) + (vmem,) * len(keep),
        out_shape=(jax.ShapeDtypeStruct((2, 1, ch, band), jnp.float32),)
        + (product_shape(ch),) * len(keep),
        scratch_shapes=[
            pltpu.VMEM((depth, ch), jnp.bfloat16),
            pltpu.VMEM((count,) + product_shape(ch).shape, jnp.float32),
            pltpu.VMEM((2, ch, (count - 1) * ch), jnp.float32),
            pltpu.SemaphoreType.DMA((2, 2)),
        ],
        input_output_aliases={} if fresh else {count + 1: 0},
        compiler_params=pltpu.CompilerParams(vmem_limit_bytes=24 * 1024 * 1024),
        cost_estimate=pl.CostEstimate(flops=0, bytes_accessed=3 << 20, transcendentals=0),
        name="region",
    )(left, *blocks, *([] if fresh else [out]))


def cross_all(blocks):
    own, first, second, third, fourth = blocks
    _, pieces, lanes = own.shape
    band = (len(blocks) - 1) * pieces * lanes // 2
    left, own_product = own_terms(own)
    out, third_product = region(left, [third, fourth], 3, band, keep=(0,))
    out, first_product = region(left, [own_product, first], 0, band, out, keep=(1,))
    out, = region(left, [first_product, second, third_product], 1, band, out)
    return out


def upper_blocks(own):
    chan = ("z", "x")
    count = lax.axis_size(chan)
    half = count // 2

    def moved(array, pairs):
        return lax.ppermute(array, chan, pairs)

    fourth = moved(own, [(c, c - half) for c in range(half, count)])
    third = moved(own, [(c, c - 3) for c in range(3, count)])
    first = moved(own, [(c, c - 1) for c in range(1, count)])
    handed = jnp.where(lax.axis_index(chan) < 2, fourth, own)
    second = moved(
        handed,
        [(c, c - 2) for c in range(2, count) if c // half == (c - 2) // half]
        + [(c, c + 2) for c in range(2)],
    )
    return [first, second, third, fourth]


def shards(record):
    core = lax.axis_index("core").astype(jnp.int32).reshape(1)
    keep, send = whitened_bins(core, record)
    got = lax.ppermute(send, "core", [(0, 1), (1, 0)])
    pairs = jnp.concatenate([keep, got], axis=1)
    own = lax.all_to_all(pairs, ("y", "zh"), split_axis=0, concat_axis=0, tiled=True)
    own = own.reshape(NBIN, keep.shape[1], LANES)
    return cross_all([own] + upper_blocks(own))


def solution(mesh):
    freq, chan = mesh.devices.shape
    devices = mesh.devices.reshape(8, freq // 16, 2, 2, chan // 2)
    fine = Mesh(devices, ("y", "zh", "core", "z", "x"))
    return jax.shard_map(
        shards,
        mesh=fine,
        in_specs=(P(("y", "zh", "core"), None, ("z", "x")),),
        out_specs=P(None, ("y", "zh", "core"), ("z", "x"), None),
        check_vma=False,
    )
```

time: 51.6 us -> 53 us (1.027)
  the two profiles are of different devices: /device:TPU:4 before, /device:TPU:2 now
where the time goes in v2:
time: 53 us; the launch traced here: 52.8 us
  blocking collectives  28.3 us (53%)
  starting transfers between devices  9.7 us (18%)
  Pallas kernels  8.19 us (15%)
  waiting for transfers between devices  6.42 us (12%)
    all_to_all x1, blocking collectives, shards(): lax.all_to_all(pairs, ('y', 'zh'), split_axis=0, concat_axis=0, tiled=True)  28.3 us
    ppermute x4, starting transfers between devices, moved(): return lax.ppermute(array, chan, pairs)  7.78 us
    ppermute x4, waiting for transfers between devices, moved(): return lax.ppermute(array, chan, pairs)  5.2 us
    pallas_call x3, Pallas kernels, region(): pl.pallas_call(functools.partial(region_kernel, first, given, keep, fresh...  4.72 us
    pallas_call x1, Pallas kernels, whitened_bins(): pl.pallas_call(functools.partial(whiten_kernel, samples), in_specs=[pl.Bl...  3.01 us
    ppermute x1, starting transfers between devices, shards(): got = lax.ppermute(send, 'core', [(0, 1), (1, 0)])  1.92 us
    ppermute x1, waiting for transfers between devices, shards(): got = lax.ppermute(send, 'core', [(0, 1), (1, 0)])  1.22 us
  transfers between devices with their start and end apart: 5, of which 3 were waited for; matrix products, arithmetic and copies ran while one was open for 0% of the time, Pallas kernels for 6%

profile of v2, /device:TPU:2, one launch (start us, length us, event | category | flops | bytes accessed | tf_op | source)
XLA Modules:
  0.0 52.8 jit_solution(11550483559116528076)
XLA Ops:
  0.0 3.0 %whiten.1 = (f32[32,4,128]{2,1,0:T(4,128)S(1)}, f32[32,4,128]{2,1,0:T(4,128)S(1)}) custom-call(s32[1]{0:T(128)} %bitcast.core_ref, bf16[1,6144,256]{2,1,0:T(8,128)(2,1)} %record_ref.1), custom_call_target="tpu_custom_call" | custom-call | tf_op jit(solution)/shard_map/whiten/pallas_call | solution.py:89
  3.0 1.9 %collective-permute-start = (f32[32,4,128]{2,1,0:T(4,128)S(1)}, f32[32,4,128]{2,1,0:T(4,128)S(1)}, u32[]{:S(2)}, u32[]{:S(2)}) collective-permute-start(f32[32,4,128]{2,1,0:T(4,128)S(1)} %get-tuple-element.14), channel_id=1, source_target_pairs={{0,8},{8,0},{1,9},{9,1},{2,10},{10,2},{3,11},{11,3},{4,12},{12,4},... | collective-permute-start | bytes 196616 | tf_op jit(solution)/shard_map/ppermute | solution.py:277
  4.9 1.2 %collective-permute-done = f32[32,4,128]{2,1,0:T(4,128)S(1)} collective-permute-done((f32[32,4,128]{2,1,0:T(4,128)S(1)}, f32[32,4,128]{2,1,0:T(4,128)S(1)}, u32[]{:S(2)}, u32[]{:S(2)}) %collective-permute-start) | collective-permute-done | bytes 65568 | tf_op jit(solution)/shard_map/ppermute | solution.py:277
  6.2 28.3 %all_to_all.5 = f32[32,8,128]{2,1,0:T(8,128)S(1)} all-to-all(f32[32,8,128]{2,1,0:T(8,128)S(1)} %pad_maximum_fusion), channel_id=1, replica_groups=mesh['y'=8,'zh'=4,'core'=2,'z'=2,'x'=4] {'y','zh'}, dimensions={0} | all-to-all | bytes 262144 | tf_op jit(solution)/shard_map/all_to_all | solution.py:279
  34.5 1.3 %collective-permute-start.3 = (f32[64,4,128]{2,1,0:T(4,128)S(1)}, f32[64,4,128]{2,1,0:T(4,128)S(1)}, u32[]{:S(2)}, u32[]{:S(2)}) collective-permute-start(f32[64,4,128]{2,1,0:T(4,128)S(1)} %bitcast.5), channel_id=1, source_target_pairs={{4,0},{5,1},{6,2},{7,3},{12,8},{13,9},{14,10},{15,11},{20,16},{21,... | collective-permute-start | bytes 393224 | tf_op jit(solution)/shard_map/ppermute | solution.py:260
  35.8 1.3 %collective-permute-start.2 = (f32[64,4,128]{2,1,0:T(4,128)S(1)}, f32[64,4,128]{2,1,0:T(4,128)S(1)}, u32[]{:S(2)}, u32[]{:S(2)}) collective-permute-start(f32[64,4,128]{2,1,0:T(4,128)S(1)} %bitcast.6), channel_id=1, source_target_pairs={{3,0},{4,1},{5,2},{6,3},{7,4},{11,8},{12,9},{13,10},{14,11},{15,12... | collective-permute-start | bytes 393224 | tf_op jit(solution)/shard_map/ppermute | solution.py:260
  37.1 2.4 %collective-permute-start.1 = (f32[64,4,128]{2,1,0:T(4,128)S(1)}, f32[64,4,128]{2,1,0:T(4,128)S(1)}, u32[]{:S(2)}, u32[]{:S(2)}) collective-permute-start(f32[64,4,128]{2,1,0:T(4,128)S(1)} %bitcast.7), channel_id=1, source_target_pairs={{1,0},{2,1},{3,2},{4,3},{5,4},{6,5},{7,6},{9,8},{10,9},{11,10},{12... | collective-permute-start | bytes 393224 | tf_op jit(solution)/shard_map/ppermute | solution.py:260
  39.6 3.1 %collective-permute-done.3.refs_1_ = f32[64,4,128]{2,1,0:T(4,128)S(1)} collective-permute-done((f32[64,4,128]{2,1,0:T(4,128)S(1)}, f32[64,4,128]{2,1,0:T(4,128)S(1)}, u32[]{:S(2)}, u32[]{:S(2)}) %collective-permute-start.3) | collective-permute-done | bytes 131104 | tf_op jit(solution)/shard_map/ppermute | solution.py:260
  42.7 2.8 %collective-permute-start.4 = (f32[64,4,128]{2,1,0:T(4,128)S(1)}, f32[64,4,128]{2,1,0:T(4,128)S(1)}, u32[]{:S(2)}, u32[]{:S(2)}) collective-permute-start(f32[64,4,128]{2,1,0:T(4,128)S(1)} %bitcast.10), channel_id=1, source_target_pairs={{2,0},{3,1},{6,4},{7,5},{0,2},{1,3},{10,8},{11,9},{14,12},{15,13},... | collective-permute-start | bytes 393224 | tf_op jit(solution)/shard_map/ppermute | solution.py:260
  45.4 0.5 own.1
  45.9 0.0 collective-permute-done.2.refs_0_
  45.9 1.6 %region.3 = (f32[2,1,256,1024]{3,2,1,0:T(8,128)}, f32[2,2,128,256]{3,2,1,0:T(8,128)S(1)}) custom-call(bf16[512,384]{1,0:T(8,128)(2,1)S(1)} %get-tuple-element.15.left_ref, f32[64,4,128]{2,1,0:T(4,128)S(1)} %collective-permute-done.2.refs_0_, f32[64,4,128]{2,1,0:T(4,128)S(1)} %collective-permute-done.3.refs_1_), custom_call_target="tpu_custom_call" | custom-call | bytes 3145728 | tf_op jit(solution)/shard_map/region/pallas_call | solution.py:224
  47.5 0.0 collective-permute-done.1.refs_1_
  47.5 1.4 %region.4 = (f32[2,1,256,1024]{3,2,1,0:T(8,128)}, f32[2,2,128,256]{3,2,1,0:T(8,128)S(1)}) custom-call(bf16[512,384]{1,0:T(8,128)(2,1)S(1)} %get-tuple-element.15.left_ref, f32[2,2,128,256]{3,2,1,0:T(8,128)S(1)} %get-tuple-element.16.refs_0_, f32[64,4,128]{2,1,0:T(4,128)S(1)} %collective-permute-done.1.refs_1_, ...), custom_call_target="tpu_custom_call", output_to_operand_aliasing={{0}: (3, {})} | custom-call | bytes 3145728 | tf_op jit(solution)/shard_map/region/pallas_call | solution.py:224
  48.9 2.1 %collective-permute-done.4.refs_1_ = f32[64,4,128]{2,1,0:T(4,128)S(1)} collective-permute-done((f32[64,4,128]{2,1,0:T(4,128)S(1)}, f32[64,4,128]{2,1,0:T(4,128)S(1)}, u32[]{:S(2)}, u32[]{:S(2)}) %collective-permute-start.4) | collective-permute-done | bytes 131104 | tf_op jit(solution)/shard_map/ppermute | solution.py:260
  51.0 1.8 %region.5 = f32[2,1,256,1024]{3,2,1,0:T(8,128)} custom-call(bf16[512,384]{1,0:T(8,128)(2,1)S(1)} %get-tuple-element.15.left_ref, f32[2,2,128,256]{3,2,1,0:T(8,128)S(1)} %get-tuple-element.18.refs_0_, f32[64,4,128]{2,1,0:T(4,128)S(1)} %collective-permute-done.4.refs_1_, ...), custom_call_target="tpu_custom_call", output_to_operand_aliasing={{}: (4, {})} | custom-call | bytes 3145728 | tf_op jit(solution)/shard_map/region/pallas_call | solution.py:224
  (2 shorter events, 0.0 us)
Async XLA Ops:
  3.0 3.1 %collective-permute-start = (f32[32,4,128]{2,1,0:T(4,128)S(1)}, f32[32,4,128]{2,1,0:T(4,128)S(1)}, u32[]{:S(2)}, u32[]{:S(2)}) collective-permute-start(f32[32,4,128]{2,1,0:T(4,128)S(1)} %get-tuple-element.14), channel_id=1, source_target_pairs={{0,8},{8,0},{1,9},{9,1},{2,10},{10,2},{3,11},{11,3},{4,12},{12,4},... | collective-permute-start | bytes 196616 | tf_op jit(solution)/shard_map/ppermute | solution.py:277
  34.5 8.1 %collective-permute-start.3 = (f32[64,4,128]{2,1,0:T(4,128)S(1)}, f32[64,4,128]{2,1,0:T(4,128)S(1)}, u32[]{:S(2)}, u32[]{:S(2)}) collective-permute-start(f32[64,4,128]{2,1,0:T(4,128)S(1)} %bitcast.5), channel_id=1, source_target_pairs={{4,0},{5,1},{6,2},{7,3},{12,8},{13,9},{14,10},{15,11},{20,16},{21,... | collective-permute-start | bytes 393224 | tf_op jit(solution)/shard_map/ppermute | solution.py:260
  35.8 10.1 %collective-permute-start.2 = (f32[64,4,128]{2,1,0:T(4,128)S(1)}, f32[64,4,128]{2,1,0:T(4,128)S(1)}, u32[]{:S(2)}, u32[]{:S(2)}) collective-permute-start(f32[64,4,128]{2,1,0:T(4,128)S(1)} %bitcast.6), channel_id=1, source_target_pairs={{3,0},{4,1},{5,2},{6,3},{7,4},{11,8},{12,9},{13,10},{14,11},{15,12... | collective-permute-start | bytes 393224 | tf_op jit(solution)/shard_map/ppermute | solution.py:260
  37.1 10.4 %collective-permute-start.1 = (f32[64,4,128]{2,1,0:T(4,128)S(1)}, f32[64,4,128]{2,1,0:T(4,128)S(1)}, u32[]{:S(2)}, u32[]{:S(2)}) collective-permute-start(f32[64,4,128]{2,1,0:T(4,128)S(1)} %bitcast.7), channel_id=1, source_target_pairs={{1,0},{2,1},{3,2},{4,3},{5,4},{6,5},{7,6},{9,8},{10,9},{11,10},{12... | collective-permute-start | bytes 393224 | tf_op jit(solution)/shard_map/ppermute | solution.py:260
  42.7 8.4 %collective-permute-start.4 = (f32[64,4,128]{2,1,0:T(4,128)S(1)}, f32[64,4,128]{2,1,0:T(4,128)S(1)}, u32[]{:S(2)}, u32[]{:S(2)}) collective-permute-start(f32[64,4,128]{2,1,0:T(4,128)S(1)} %bitcast.10), channel_id=1, source_target_pairs={{2,0},{3,1},{6,4},{7,5},{0,2},{1,3},{10,8},{11,9},{14,12},{15,13},... | collective-permute-start | bytes 393224 | tf_op jit(solution)/shard_map/ppermute | solution.py:260

commit v3 on v2

--- a/solution.py
+++ b/solution.py
@@ -6,39 +6,48 @@
 from jax import lax
 from jax.experimental import pallas as pl
 from jax.experimental.pallas import tpu as pltpu
-from jax.sharding import Mesh, PartitionSpec as P
+from jax.sharding import PartitionSpec as P
 
 NBIN = 64
 NEIGH = 40
-CHUNKS = 4
+CHUNKS = 6
 ROWS = 64
 LANES = 128
 
 
-def bin_of(row):
-    return 2 * (row & (NBIN // 2 - 1)) + row // (NBIN // 2)
-
-
-def neighbour_weights():
-    row = bin_of(lax.broadcasted_iota(jnp.int32, (NBIN, NBIN), 0))
-    col = bin_of(lax.broadcasted_iota(jnp.int32, (NBIN, NBIN), 1))
+def split_terms(x, rest=jnp.bfloat16):
+    high = x.astype(jnp.bfloat16)
+    return high, (x - high.astype(jnp.float32)).astype(rest)
+
+
+def smoothed(power):
+    row = lax.broadcasted_iota(jnp.int32, (NBIN, NBIN), 0)
+    col = lax.broadcasted_iota(jnp.int32, (NBIN, NBIN), 1)
     below, above = NEIGH // 2, NEIGH - NEIGH // 2
-    inside = (col - row >= -below) & (col - row < above)
-    count = jnp.minimum(row + above, NBIN) - jnp.maximum(row - below, 0)
-    return jnp.where(inside, 1.0 / count.astype(jnp.float32), 0.0)
+    inside = ((col - row >= -below) & (col - row < above)).astype(jnp.float32)
+    inside = inside.astype(jnp.bfloat16)
+    high, rest = split_terms(power, jnp.float32)
+    middle, low = split_terms(rest, jnp.bfloat16)
+    total = jnp.dot(
+        jnp.concatenate([inside, inside, inside], axis=1),
+        jnp.concatenate([high, middle, low], axis=0),
+        preferred_element_type=jnp.float32,
+    )
+    first = lax.broadcasted_iota(jnp.int32, power.shape, 0)
+    count = jnp.minimum(first + above, NBIN) - jnp.maximum(first - below, 0)
+    return total / count.astype(jnp.float32)
 
 
 def base_angles(samples):
     stride, period = samples // (2 * NBIN), 2 * NBIN
-    k = bin_of(lax.broadcasted_iota(jnp.int32, (NBIN, period), 0))
+    k = lax.broadcasted_iota(jnp.int32, (NBIN, period), 0)
     s = lax.broadcasted_iota(jnp.int32, (NBIN, period), 1)
     phase = s + stride * ((k * s) & (period - 1))
     return 2.0 * math.pi / samples * phase.astype(jnp.float32)
 
 
-def whiten_kernel(samples, core_ref, record_ref, keep_ref, send_ref, buf_ref, table_ref, sems):
+def whiten_kernel(samples, record_ref, out_ref, buf_ref, table_ref, sems):
     chunk = samples // CHUNKS
-    quarter = samples // 4
     period = 2 * NBIN
     turns = samples // period
 
@@ -47,66 +56,46 @@
         return pltpu.make_async_copy(record_ref.at[0, part], buf_ref.at[part], sems.at[n])
 
     for n in range(CHUNKS):
-        fetch(n).start(priority=n % 2)
+        fetch(n).start()
     angle = base_angles(samples)
     cos, sin = jnp.cos(angle), jnp.sin(angle)
-    for m in range(quarter // period):
+    for m in range(turns):
         c, s = math.cos(2.0 * math.pi * m / turns), math.sin(2.0 * math.pi * m / turns)
         part = pl.ds(m * period, period)
         table_ref[:NBIN, part] = (c * cos - s * sin).astype(jnp.bfloat16)
-        table_ref[NBIN:, part] = (-s * cos - c * sin).astype(jnp.bfloat16)
-    sums = [None] * 4
+        table_ref[NBIN:, part] = (-(s * cos + c * sin)).astype(jnp.bfloat16)
+    total = None
     for n in range(CHUNKS):
         fetch(n).wait()
-        q, start = divmod(n * chunk, quarter)
-        term = jnp.dot(table_ref[:, pl.ds(start, chunk)], buf_ref[pl.ds(n * chunk, chunk)],
-                       preferred_element_type=jnp.float32)
-        sums[q] = term if sums[q] is None else sums[q] + term
-    even, odd = sums[0] - sums[2], sums[1] - sums[3]
+        part = pl.ds(n * chunk, chunk)
+        term = jnp.dot(table_ref[:, part], buf_ref[part], preferred_element_type=jnp.float32)
+        total = term if total is None else total + term
     scaling = 1.0 / math.sqrt(samples)
-    re = (even[:NBIN] + odd[NBIN:]) * scaling
-    im = (even[NBIN:] - odd[:NBIN]) * scaling
+    re, im = total[:NBIN] * scaling, total[NBIN:] * scaling
     power = 0.5 * (re * re + im * im)
-    smooth = jnp.dot(neighbour_weights(), power, precision=lax.Precision.HIGHEST,
-                     preferred_element_type=jnp.float32)
-    gain = lax.rsqrt(smooth + 1e-06)
-    re, im = re * gain, im * gain
-    even_core = core_ref[0] == 0
-    pieces = re.shape[1] // LANES
-    for p, value in enumerate((re, im)):
-        lower, upper = value[:NBIN // 2], value[NBIN // 2:]
-        keep, send = jnp.where(even_core, lower, upper), jnp.where(even_core, upper, lower)
-        for n in range(pieces):
-            part = slice(n * LANES, (n + 1) * LANES)
-            keep_ref[:, p * pieces + n, :] = keep[:, part]
-            send_ref[:, p * pieces + n, :] = send[:, part]
-
-
-def whitened_bins(core, record):
+    gain = lax.rsqrt(smoothed(power) + 1e-06)
+    half = re.shape[1] // LANES
+    for n in range(half):
+        part = slice(n * LANES, (n + 1) * LANES)
+        out_ref[:, n, :] = (re * gain)[:, part]
+        out_ref[:, half + n, :] = (im * gain)[:, part]
+
+
+def whitened_bins(record):
     _, samples, ch = record.shape
-    vmem = pl.BlockSpec(memory_space=pltpu.VMEM)
-    shape = jax.ShapeDtypeStruct((NBIN // 2, 2 * ch // LANES, LANES), jnp.float32)
     return pl.pallas_call(
         functools.partial(whiten_kernel, samples),
-        in_specs=[
-            pl.BlockSpec(memory_space=pltpu.SMEM),
-            pl.BlockSpec(memory_space=pltpu.HBM),
-        ],
-        out_specs=(vmem, vmem),
-        out_shape=(shape, shape),
+        in_specs=[pl.BlockSpec(memory_space=pltpu.HBM)],
+        out_specs=pl.BlockSpec(memory_space=pltpu.VMEM),
+        out_shape=jax.ShapeDtypeStruct((NBIN, 2 * ch // LANES, LANES), jnp.float32),
         scratch_shapes=[
             pltpu.VMEM((samples, ch), jnp.bfloat16),
-            pltpu.VMEM((2 * NBIN, samples // 4), jnp.bfloat16),
+            pltpu.VMEM((2 * NBIN, samples), jnp.bfloat16),
             pltpu.SemaphoreType.DMA((CHUNKS,)),
         ],
         compiler_params=pltpu.CompilerParams(vmem_limit_bytes=52 * 1024 * 1024),
         name="whiten",
-    )(core, record)
-
-
-def split_terms(x):
-    high = x.astype(jnp.bfloat16)
-    return high, (x - high.astype(jnp.float32)).astype(jnp.bfloat16)
+    )(record)
 
 
 def real_imag(block_ref):
@@ -246,49 +235,28 @@
     band = (len(blocks) - 1) * pieces * lanes // 2
     left, own_product = own_terms(own)
     out, third_product = region(left, [third, fourth], 3, band, keep=(0,))
-    out, first_product = region(left, [own_product, first], 0, band, out, keep=(1,))
-    out, = region(left, [first_product, second, third_product], 1, band, out)
+    out, second_product = region(left, [second, third_product], 2, band, out, keep=(0,))
+    out, = region(left, [own_product, first, second_product], 0, band, out)
     return out
 
 
-def upper_blocks(own):
-    chan = ("z", "x")
-    count = lax.axis_size(chan)
-    half = count // 2
-
-    def moved(array, pairs):
-        return lax.ppermute(array, chan, pairs)
-
-    fourth = moved(own, [(c, c - half) for c in range(half, count)])
-    third = moved(own, [(c, c - 3) for c in range(3, count)])
-    first = moved(own, [(c, c - 1) for c in range(1, count)])
-    handed = jnp.where(lax.axis_index(chan) < 2, fourth, own)
-    second = moved(
-        handed,
-        [(c, c - 2) for c in range(2, count) if c // half == (c - 2) // half]
-        + [(c, c + 2) for c in range(2)],
-    )
-    return [first, second, third, fourth]
+def upper_block(own, offset):
+    count = lax.axis_size("chan")
+    return lax.ppermute(own, "chan", [(c, c - offset) for c in range(offset, count)])
 
 
 def shards(record):
-    core = lax.axis_index("core").astype(jnp.int32).reshape(1)
-    keep, send = whitened_bins(core, record)
-    got = lax.ppermute(send, "core", [(0, 1), (1, 0)])
-    pairs = jnp.concatenate([keep, got], axis=1)
-    own = lax.all_to_all(pairs, ("y", "zh"), split_axis=0, concat_axis=0, tiled=True)
-    own = own.reshape(NBIN, keep.shape[1], LANES)
-    return cross_all([own] + upper_blocks(own))
+    bins = whitened_bins(record)
+    own = lax.all_to_all(bins, "freq", split_axis=0, concat_axis=0, tiled=True)
+    reach = lax.axis_size("chan") // 2
+    return cross_all([own] + [upper_block(own, offset) for offset in range(1, reach + 1)])
 
 
 def solution(mesh):
-    freq, chan = mesh.devices.shape
-    devices = mesh.devices.reshape(8, freq // 16, 2, 2, chan // 2)
-    fine = Mesh(devices, ("y", "zh", "core", "z", "x"))
     return jax.shard_map(
         shards,
-        mesh=fine,
-        in_specs=(P(("y", "zh", "core"), None, ("z", "x")),),
-        out_specs=P(None, ("y", "zh", "core"), ("z", "x"), None),
+        mesh=mesh,
+        in_specs=(P("freq", None, "chan"),),
+        out_specs=P(None, "freq", "chan", None),
         check_vma=False,
     )

time: 53 us -> 51.2 us (0.966)
  the two profiles are of different devices: /device:TPU:2 before, /device:TPU:6 now
where the time goes in v3:
time: 51.2 us; the launch traced here: 51 us
  blocking collectives  29.8 us (58%)
  Pallas kernels  7.81 us (15%)
  starting transfers between devices  7.81 us (15%)
  waiting for transfers between devices  5.49 us (11%)
    all_to_all x1, blocking collectives, shards(): own = lax.all_to_all(bins, 'freq', split_axis=0, concat_axis=0, tiled=True)  29.8 us
    ppermute x4, starting transfers between devices, upper_block(): lax.ppermute(own, 'chan', [(c, c - offset) for c in range(offset, count)])  7.81 us
    ppermute x4, waiting for transfers between devices, upper_block(): lax.ppermute(own, 'chan', [(c, c - offset) for c in range(offset, count)])  5.49 us
    pallas_call x3, Pallas kernels, region(): pl.pallas_call(functools.partial(region_kernel, first, given, keep, fresh...  4.71 us
    pallas_call x1, Pallas kernels, whitened_bins(): pl.pallas_call(functools.partial(whiten_kernel, samples), in_specs=[pl.Bl...  2.65 us
  transfers between devices with their start and end apart: 4, of which 3 were waited for; matrix products, arithmetic and copies ran while one was open for 0% of the time, Pallas kernels for 7%

profile of v3, /device:TPU:6, one launch (start us, length us, event | category | flops | bytes accessed | tf_op | source)
XLA Modules:
  0.0 51.0 jit_solution(7015348644315931901)
XLA Ops:
  0.0 2.6 %whiten.1 = f32[64,4,128]{2,1,0:T(4,128)S(1)} custom-call(bf16[1,6144,256]{2,1,0:T(8,128)(2,1)} %record_ref.1), custom_call_target="tpu_custom_call" | custom-call | tf_op jit(solution)/shard_map/whiten/pallas_call | solution.py:86
  2.7 29.8 %all_to_all.5.own_ref = f32[64,4,128]{2,1,0:T(4,128)S(1)} all-to-all(f32[64,4,128]{2,1,0:T(4,128)S(1)} %whiten.1), channel_id=1, replica_groups=mesh['freq'=64,'chan'=8] {'freq'}, dimensions={0} | all-to-all | bytes 262144 | tf_op jit(solution)/shard_map/all_to_all | solution.py:250
  32.5 1.3 %collective-permute-start.3 = (f32[64,4,128]{2,1,0:T(4,128)S(1)}, f32[64,4,128]{2,1,0:T(4,128)S(1)}, u32[]{:S(2)}, u32[]{:S(2)}) collective-permute-start(f32[64,4,128]{2,1,0:T(4,128)S(1)} %all_to_all.5.own_ref), channel_id=1, source_target_pairs={{4,0},{5,1},{6,2},{7,3},{12,8},{13,9},{14,10},{15,11},{20,16},{21,... | collective-permute-start | bytes 393224 | tf_op jit(solution)/shard_map/ppermute | solution.py:245
  33.8 2.4 %collective-permute-start.2 = (f32[64,4,128]{2,1,0:T(4,128)S(1)}, f32[64,4,128]{2,1,0:T(4,128)S(1)}, u32[]{:S(2)}, u32[]{:S(2)}) collective-permute-start(f32[64,4,128]{2,1,0:T(4,128)S(1)} %all_to_all.5.own_ref), channel_id=1, source_target_pairs={{3,0},{4,1},{5,2},{6,3},{7,4},{11,8},{12,9},{13,10},{14,11},{15,12... | collective-permute-start | bytes 393224 | tf_op jit(solution)/shard_map/ppermute | solution.py:245
  36.2 2.2 %collective-permute-start.1 = (f32[64,4,128]{2,1,0:T(4,128)S(1)}, f32[64,4,128]{2,1,0:T(4,128)S(1)}, u32[]{:S(2)}, u32[]{:S(2)}) collective-permute-start(f32[64,4,128]{2,1,0:T(4,128)S(1)} %all_to_all.5.own_ref), channel_id=1, source_target_pairs={{2,0},{3,1},{4,2},{5,3},{6,4},{7,5},{10,8},{11,9},{12,10},{13,11},... | collective-permute-start | bytes 393224 | tf_op jit(solution)/shard_map/ppermute | solution.py:245
  38.4 1.9 %collective-permute-start = (f32[64,4,128]{2,1,0:T(4,128)S(1)}, f32[64,4,128]{2,1,0:T(4,128)S(1)}, u32[]{:S(2)}, u32[]{:S(2)}) collective-permute-start(f32[64,4,128]{2,1,0:T(4,128)S(1)} %all_to_all.5.own_ref), channel_id=1, source_target_pairs={{1,0},{2,1},{3,2},{4,3},{5,4},{6,5},{7,6},{9,8},{10,9},{11,10},{12... | collective-permute-start | bytes 393224 | tf_op jit(solution)/shard_map/ppermute | solution.py:245
  40.3 0.5 own.1
  40.8 0.0 collective-permute-done.3.refs_1_
  40.8 2.3 %collective-permute-done.2.refs_0_ = f32[64,4,128]{2,1,0:T(4,128)S(1)} collective-permute-done((f32[64,4,128]{2,1,0:T(4,128)S(1)}, f32[64,4,128]{2,1,0:T(4,128)S(1)}, u32[]{:S(2)}, u32[]{:S(2)}) %collective-permute-start.2) | collective-permute-done | bytes 131104 | tf_op jit(solution)/shard_map/ppermute | solution.py:245
  43.1 1.6 %region.3 = (f32[2,1,256,1024]{3,2,1,0:T(8,128)}, f32[2,2,128,256]{3,2,1,0:T(8,128)S(1)}) custom-call(bf16[512,384]{1,0:T(8,128)(2,1)S(1)} %get-tuple-element.11.left_ref, f32[64,4,128]{2,1,0:T(4,128)S(1)} %collective-permute-done.2.refs_0_, f32[64,4,128]{2,1,0:T(4,128)S(1)} %collective-permute-done.3.refs_1_), custom_call_target="tpu_custom_call" | custom-call | bytes 3145728 | tf_op jit(solution)/shard_map/region/pallas_call | solution.py:213
  44.6 2.9 %collective-permute-done.1.refs_0_ = f32[64,4,128]{2,1,0:T(4,128)S(1)} collective-permute-done((f32[64,4,128]{2,1,0:T(4,128)S(1)}, f32[64,4,128]{2,1,0:T(4,128)S(1)}, u32[]{:S(2)}, u32[]{:S(2)}) %collective-permute-start.1) | collective-permute-done | bytes 131104 | tf_op jit(solution)/shard_map/ppermute | solution.py:245
  47.6 1.4 %region.4 = (f32[2,1,256,1024]{3,2,1,0:T(8,128)}, f32[2,2,128,256]{3,2,1,0:T(8,128)S(1)}) custom-call(bf16[512,384]{1,0:T(8,128)(2,1)S(1)} %get-tuple-element.11.left_ref, f32[64,4,128]{2,1,0:T(4,128)S(1)} %collective-permute-done.1.refs_0_, f32[2,2,128,256]{3,2,1,0:T(8,128)S(1)} %get-tuple-element.13.refs_1_, ...), custom_call_target="tpu_custom_call", output_to_operand_aliasing={{0}: (3, {})} | custom-call | bytes 3145728 | tf_op jit(solution)/shard_map/region/pallas_call | solution.py:213
  49.0 0.3 collective-permute-done.refs_1_
  49.3 1.8 %region.5 = f32[2,1,256,1024]{3,2,1,0:T(8,128)} custom-call(bf16[512,384]{1,0:T(8,128)(2,1)S(1)} %get-tuple-element.11.left_ref, f32[2,2,128,256]{3,2,1,0:T(8,128)S(1)} %get-tuple-element.12.refs_0_, f32[64,4,128]{2,1,0:T(4,128)S(1)} %collective-permute-done.refs_1_, ...), custom_call_target="tpu_custom_call", output_to_operand_aliasing={{}: (4, {})} | custom-call | bytes 3145728 | tf_op jit(solution)/shard_map/region/pallas_call | solution.py:213
Async XLA Ops:
  32.5 8.3 %collective-permute-start.3 = (f32[64,4,128]{2,1,0:T(4,128)S(1)}, f32[64,4,128]{2,1,0:T(4,128)S(1)}, u32[]{:S(2)}, u32[]{:S(2)}) collective-permute-start(f32[64,4,128]{2,1,0:T(4,128)S(1)} %all_to_all.5.own_ref), channel_id=1, source_target_pairs={{4,0},{5,1},{6,2},{7,3},{12,8},{13,9},{14,10},{15,11},{20,16},{21,... | collective-permute-start | bytes 393224 | tf_op jit(solution)/shard_map/ppermute | solution.py:245
  33.8 9.3 %collective-permute-start.2 = (f32[64,4,128]{2,1,0:T(4,128)S(1)}, f32[64,4,128]{2,1,0:T(4,128)S(1)}, u32[]{:S(2)}, u32[]{:S(2)}) collective-permute-start(f32[64,4,128]{2,1,0:T(4,128)S(1)} %all_to_all.5.own_ref), channel_id=1, source_target_pairs={{3,0},{4,1},{5,2},{6,3},{7,4},{11,8},{12,9},{13,10},{14,11},{15,12... | collective-permute-start | bytes 393224 | tf_op jit(solution)/shard_map/ppermute | solution.py:245
  36.2 11.4 %collective-permute-start.1 = (f32[64,4,128]{2,1,0:T(4,128)S(1)}, f32[64,4,128]{2,1,0:T(4,128)S(1)}, u32[]{:S(2)}, u32[]{:S(2)}) collective-permute-start(f32[64,4,128]{2,1,0:T(4,128)S(1)} %all_to_all.5.own_ref), channel_id=1, source_target_pairs={{2,0},{3,1},{4,2},{5,3},{6,4},{7,5},{10,8},{11,9},{12,10},{13,11},... | collective-permute-start | bytes 393224 | tf_op jit(solution)/shard_map/ppermute | solution.py:245
  38.4 10.9 %collective-permute-start = (f32[64,4,128]{2,1,0:T(4,128)S(1)}, f32[64,4,128]{2,1,0:T(4,128)S(1)}, u32[]{:S(2)}, u32[]{:S(2)}) collective-permute-start(f32[64,4,128]{2,1,0:T(4,128)S(1)} %all_to_all.5.own_ref), channel_id=1, source_target_pairs={{1,0},{2,1},{3,2},{4,3},{5,4},{6,5},{7,6},{9,8},{10,9},{11,10},{12... | collective-permute-start | bytes 393224 | tf_op jit(solution)/shard_map/ppermute | solution.py:245

commit v4 on v3

--- a/solution.py
+++ b/solution.py
@@ -240,16 +240,27 @@
     return out
 
 
-def upper_block(own, offset):
+def upper_blocks(own):
     count = lax.axis_size("chan")
-    return lax.ppermute(own, "chan", [(c, c - offset) for c in range(offset, count)])
+    half = count // 2
+
+    def moved(array, pairs):
+        return lax.ppermute(array, "chan", pairs)
+
+    fourth, third, second = (
+        moved(own, [(c, c - by) for c in range(by, count)]) for by in (half, 3, 2)
+    )
+    handed = jnp.where(lax.axis_index("chan") == 0, fourth, own)
+    first = moved(
+        handed, [(c, c - 1) for c in range(1, count) if c != half] + [(0, half - 1)]
+    )
+    return [first, second, third, fourth]
 
 
 def shards(record):
     bins = whitened_bins(record)
     own = lax.all_to_all(bins, "freq", split_axis=0, concat_axis=0, tiled=True)
-    reach = lax.axis_size("chan") // 2
-    return cross_all([own] + [upper_block(own, offset) for offset in range(1, reach + 1)])
+    return cross_all([own] + upper_blocks(own))
 
 
 def solution(mesh):

time: 51.2 us -> 51.8 us (1.012); the launches traced: 51 us -> 51 us
  waiting for transfers between devices: 5.49 us -> 3.81 us
  starting transfers between devices: 7.81 us -> 9.46 us
    ppermute x4, waiting for transfers between devices: 5.49 us -> 3.81 us  [moved(): return lax.ppermute(array, 'chan', pairs)]
    ppermute x4, starting transfers between devices: 7.81 us -> 9.46 us  [moved(): return lax.ppermute(array, 'chan', pairs)]
where the time goes in v4:
time: 51.8 us; the launch traced here: 51 us
  blocking collectives  29.8 us (58%)
  starting transfers between devices  9.46 us (18%)
  Pallas kernels  7.82 us (15%)
  waiting for transfers between devices  3.81 us (7%)
    all_to_all x1, blocking collectives, shards(): own = lax.all_to_all(bins, 'freq', split_axis=0, concat_axis=0, tiled=True)  29.8 us
    ppermute x4, starting transfers between devices, moved(): return lax.ppermute(array, 'chan', pairs)  9.46 us
    pallas_call x3, Pallas kernels, region(): pl.pallas_call(functools.partial(region_kernel, first, given, keep, fresh...  4.71 us
    ppermute x4, waiting for transfers between devices, moved(): return lax.ppermute(array, 'chan', pairs)  3.81 us
    pallas_call x1, Pallas kernels, whitened_bins(): pl.pallas_call(functools.partial(whiten_kernel, samples), in_specs=[pl.Bl...  2.65 us
  transfers between devices with their start and end apart: 4, of which 3 were waited for; matrix products, arithmetic and copies ran while one was open for 0% of the time, Pallas kernels for 7%

profile of v4, /device:TPU:6, one launch (start us, length us, event | category | flops | bytes accessed | tf_op | source)
XLA Modules:
  0.0 51.0 jit_solution(5808110160366462773)
XLA Ops:
  0.0 2.6 %whiten.1 = f32[64,4,128]{2,1,0:T(4,128)S(1)} custom-call(bf16[1,6144,256]{2,1,0:T(8,128)(2,1)} %record_ref.1), custom_call_target="tpu_custom_call" | custom-call | tf_op jit(solution)/shard_map/whiten/pallas_call | solution.py:86
  2.7 29.8 %all_to_all.5.own_ref = f32[64,4,128]{2,1,0:T(4,128)S(1)} all-to-all(f32[64,4,128]{2,1,0:T(4,128)S(1)} %whiten.1), channel_id=1, replica_groups=mesh['freq'=64,'chan'=8] {'freq'}, dimensions={0} | all-to-all | bytes 262144 | tf_op jit(solution)/shard_map/all_to_all | solution.py:262
  32.5 1.3 %collective-permute-start = (f32[64,4,128]{2,1,0:T(4,128)S(1)}, f32[64,4,128]{2,1,0:T(4,128)S(1)}, u32[]{:S(2)}, u32[]{:S(2)}) collective-permute-start(f32[64,4,128]{2,1,0:T(4,128)S(1)} %all_to_all.5.own_ref), channel_id=1, source_target_pairs={{4,0},{5,1},{6,2},{7,3},{12,8},{13,9},{14,10},{15,11},{20,16},{21,... | collective-permute-start | bytes 393224 | tf_op jit(solution)/shard_map/ppermute | solution.py:248
  33.8 2.4 %collective-permute-start.3 = (f32[64,4,128]{2,1,0:T(4,128)S(1)}, f32[64,4,128]{2,1,0:T(4,128)S(1)}, u32[]{:S(2)}, u32[]{:S(2)}) collective-permute-start(f32[64,4,128]{2,1,0:T(4,128)S(1)} %all_to_all.5.own_ref), channel_id=1, source_target_pairs={{3,0},{4,1},{5,2},{6,3},{7,4},{11,8},{12,9},{13,10},{14,11},{15,12... | collective-permute-start | bytes 393224 | tf_op jit(solution)/shard_map/ppermute | solution.py:248
  36.2 2.2 %collective-permute-start.2 = (f32[64,4,128]{2,1,0:T(4,128)S(1)}, f32[64,4,128]{2,1,0:T(4,128)S(1)}, u32[]{:S(2)}, u32[]{:S(2)}) collective-permute-start(f32[64,4,128]{2,1,0:T(4,128)S(1)} %all_to_all.5.own_ref), channel_id=1, source_target_pairs={{2,0},{3,1},{4,2},{5,3},{6,4},{7,5},{10,8},{11,9},{12,10},{13,11},... | collective-permute-start | bytes 393224 | tf_op jit(solution)/shard_map/ppermute | solution.py:248
  38.4 1.5 %collective-permute-done.refs_1_ = f32[64,4,128]{2,1,0:T(4,128)S(1)} collective-permute-done((f32[64,4,128]{2,1,0:T(4,128)S(1)}, f32[64,4,128]{2,1,0:T(4,128)S(1)}, u32[]{:S(2)}, u32[]{:S(2)}) %collective-permute-start) | collective-permute-done | bytes 131104 | tf_op jit(solution)/shard_map/ppermute | solution.py:248
  39.9 3.6 %collective-permute-start.1 = (f32[64,4,128]{2,1,0:T(4,128)S(1)}, f32[64,4,128]{2,1,0:T(4,128)S(1)}, u32[]{:S(2)}, u32[]{:S(2)}) collective-permute-start(f32[64,4,128]{2,1,0:T(4,128)S(1)} %bitcast.5), channel_id=1, source_target_pairs={{1,0},{2,1},{3,2},{5,4},{6,5},{7,6},{0,3},{9,8},{10,9},{11,10},{13... | collective-permute-start | bytes 393224 | tf_op jit(solution)/shard_map/ppermute | solution.py:248
  43.5 0.5 own.1
  44.0 0.0 collective-permute-done.3.refs_0_
  44.0 1.6 %region.3 = (f32[2,1,256,1024]{3,2,1,0:T(8,128)}, f32[2,2,128,256]{3,2,1,0:T(8,128)S(1)}) custom-call(bf16[512,384]{1,0:T(8,128)(2,1)S(1)} %get-tuple-element.11.left_ref, f32[64,4,128]{2,1,0:T(4,128)S(1)} %collective-permute-done.3.refs_0_, f32[64,4,128]{2,1,0:T(4,128)S(1)} %collective-permute-done.refs_1_), custom_call_target="tpu_custom_call" | custom-call | bytes 3145728 | tf_op jit(solution)/shard_map/region/pallas_call | solution.py:213
  45.5 1.0 %collective-permute-done.2.refs_0_ = f32[64,4,128]{2,1,0:T(4,128)S(1)} collective-permute-done((f32[64,4,128]{2,1,0:T(4,128)S(1)}, f32[64,4,128]{2,1,0:T(4,128)S(1)}, u32[]{:S(2)}, u32[]{:S(2)}) %collective-permute-start.2) | collective-permute-done | bytes 131104 | tf_op jit(solution)/shard_map/ppermute | solution.py:248
  46.6 1.4 %region.4 = (f32[2,1,256,1024]{3,2,1,0:T(8,128)}, f32[2,2,128,256]{3,2,1,0:T(8,128)S(1)}) custom-call(bf16[512,384]{1,0:T(8,128)(2,1)S(1)} %get-tuple-element.11.left_ref, f32[64,4,128]{2,1,0:T(4,128)S(1)} %collective-permute-done.2.refs_0_, f32[2,2,128,256]{3,2,1,0:T(8,128)S(1)} %get-tuple-element.13.refs_1_, ...), custom_call_target="tpu_custom_call", output_to_operand_aliasing={{0}: (3, {})} | custom-call | bytes 3145728 | tf_op jit(solution)/shard_map/region/pallas_call | solution.py:213
  48.0 1.3 %collective-permute-done.1.refs_1_ = f32[64,4,128]{2,1,0:T(4,128)S(1)} collective-permute-done((f32[64,4,128]{2,1,0:T(4,128)S(1)}, f32[64,4,128]{2,1,0:T(4,128)S(1)}, u32[]{:S(2)}, u32[]{:S(2)}) %collective-permute-start.1) | collective-permute-done | bytes 131104 | tf_op jit(solution)/shard_map/ppermute | solution.py:248
  49.3 1.8 %region.5 = f32[2,1,256,1024]{3,2,1,0:T(8,128)} custom-call(bf16[512,384]{1,0:T(8,128)(2,1)S(1)} %get-tuple-element.11.left_ref, f32[2,2,128,256]{3,2,1,0:T(8,128)S(1)} %get-tuple-element.12.refs_0_, f32[64,4,128]{2,1,0:T(4,128)S(1)} %collective-permute-done.1.refs_1_, ...), custom_call_target="tpu_custom_call", output_to_operand_aliasing={{}: (4, {})} | custom-call | bytes 3145728 | tf_op jit(solution)/shard_map/region/pallas_call | solution.py:213
  (1 shorter events, 0.0 us)
Async XLA Ops:
  32.5 7.4 %collective-permute-start = (f32[64,4,128]{2,1,0:T(4,128)S(1)}, f32[64,4,128]{2,1,0:T(4,128)S(1)}, u32[]{:S(2)}, u32[]{:S(2)}) collective-permute-start(f32[64,4,128]{2,1,0:T(4,128)S(1)} %all_to_all.5.own_ref), channel_id=1, source_target_pairs={{4,0},{5,1},{6,2},{7,3},{12,8},{13,9},{14,10},{15,11},{20,16},{21,... | collective-permute-start | bytes 393224 | tf_op jit(solution)/shard_map/ppermute | solution.py:248
  33.8 10.2 %collective-permute-start.3 = (f32[64,4,128]{2,1,0:T(4,128)S(1)}, f32[64,4,128]{2,1,0:T(4,128)S(1)}, u32[]{:S(2)}, u32[]{:S(2)}) collective-permute-start(f32[64,4,128]{2,1,0:T(4,128)S(1)} %all_to_all.5.own_ref), channel_id=1, source_target_pairs={{3,0},{4,1},{5,2},{6,3},{7,4},{11,8},{12,9},{13,10},{14,11},{15,12... | collective-permute-start | bytes 393224 | tf_op jit(solution)/shard_map/ppermute | solution.py:248
  36.2 10.4 %collective-permute-start.2 = (f32[64,4,128]{2,1,0:T(4,128)S(1)}, f32[64,4,128]{2,1,0:T(4,128)S(1)}, u32[]{:S(2)}, u32[]{:S(2)}) collective-permute-start(f32[64,4,128]{2,1,0:T(4,128)S(1)} %all_to_all.5.own_ref), channel_id=1, source_target_pairs={{2,0},{3,1},{4,2},{5,3},{6,4},{7,5},{10,8},{11,9},{12,10},{13,11},... | collective-permute-start | bytes 393224 | tf_op jit(solution)/shard_map/ppermute | solution.py:248
  39.9 9.4 %collective-permute-start.1 = (f32[64,4,128]{2,1,0:T(4,128)S(1)}, f32[64,4,128]{2,1,0:T(4,128)S(1)}, u32[]{:S(2)}, u32[]{:S(2)}) collective-permute-start(f32[64,4,128]{2,1,0:T(4,128)S(1)} %bitcast.5), channel_id=1, source_target_pairs={{1,0},{2,1},{3,2},{5,4},{6,5},{7,6},{0,3},{9,8},{10,9},{11,10},{13... | collective-permute-start | bytes 393224 | tf_op jit(solution)/shard_map/ppermute | solution.py:248

commit v5 on v4

--- a/solution.py
+++ b/solution.py
@@ -104,16 +104,24 @@
     return jnp.concatenate(tiles[:half], axis=1), jnp.concatenate(tiles[half:], axis=1)
 
 
-def product(left_ref, block_ref, wide_ref, out_ref):
+def spread(block_ref, wide_ref):
     re, im = real_imag(block_ref)
     high, low = split_terms(jnp.concatenate([re, im], axis=0))
     wide_ref[...] = jnp.concatenate([high, high, low], axis=0)
-    halves, parts, rows, ch = out_ref.shape
-    for a in range(halves):
-        here = pl.ds(a * parts * rows, parts * rows)
-        out_ref[a] = jnp.dot(
-            left_ref[here], wide_ref[...], preferred_element_type=jnp.float32
-        ).reshape(parts, rows, ch)
+
+
+def product(left_ref, wide_ref, out_ref, half):
+    _, parts, rows, ch = out_ref.shape
+    here = pl.ds(half * parts * rows, parts * rows)
+    out_ref[half] = jnp.dot(
+        left_ref[here], wide_ref[...], preferred_element_type=jnp.float32
+    ).reshape(parts, rows, ch)
+
+
+def product_kernel(left_ref, block_ref, prod_ref, wide_ref):
+    spread(block_ref, wide_ref)
+    for half in range(2):
+        product(left_ref, wide_ref, prod_ref, half)
 
 
 def own_kernel(own_ref, left_ref, prod_ref, wide_ref):
@@ -128,7 +136,7 @@
         )
         high, low = split_terms(left)
         left_ref[2 * a * rows:2 * (a + 1) * rows] = jnp.concatenate([high, low, high], axis=1)
-    product(left_ref, own_ref, wide_ref, prod_ref)
+    product_kernel(left_ref, own_ref, prod_ref, wide_ref)
 
 
 def product_shape(ch):
@@ -154,26 +162,40 @@
     )(own)
 
 
+def block_product(left, block):
+    rows, depth = left.shape
+    vmem = pl.BlockSpec(memory_space=pltpu.VMEM)
+    return pl.pallas_call(
+        product_kernel,
+        in_specs=[vmem, vmem],
+        out_specs=vmem,
+        out_shape=product_shape(rows // 2),
+        scratch_shapes=[pltpu.VMEM((depth, rows // 2), jnp.bfloat16)],
+        compiler_params=pltpu.CompilerParams(vmem_limit_bytes=16 * 1024 * 1024),
+        cost_estimate=pl.CostEstimate(flops=0, bytes_accessed=1 << 20, transcendentals=0),
+        name="product",
+    )(left, block)
+
+
 def region_kernel(first, given, keep, fresh, left_ref, *refs):
     count = len(given)
     blocks, refs = refs[:count], refs[count if fresh else count + 1:]
     out_ref, kept, refs = refs[0], refs[1:1 + len(keep)], refs[1 + len(keep):]
     wide_ref, prod_ref, band_ref, sems = refs
-    products = []
-    for n in range(count):
-        if given[n]:
-            products.append(blocks[n])
-            continue
-        target = kept[keep.index(n)] if n in keep else prod_ref.at[n]
-        product(left_ref, blocks[n], wide_ref, target)
-        products.append(target)
-    ch = wide_ref.shape[1]
+    products = list(blocks)
+    fresh_blocks = [n for n in range(count) if not given[n]]
+    for n in fresh_blocks:
+        spread(blocks[n], wide_ref.at[n])
+        products[n] = kept[keep.index(n)] if n in keep else prod_ref.at[n]
+    ch = wide_ref.shape[2]
     rows = ch // 2
     tiles = ch // LANES
     row = lax.broadcasted_iota(jnp.int32, (ROWS, LANES), 0)
     lane = lax.broadcasted_iota(jnp.int32, (ROWS, LANES), 1)
     copies = []
     for a in range(2):
+        for n in fresh_blocks:
+            product(left_ref, wide_ref.at[n], products[n], a)
         for part in range(2):
             for start in range(0, rows, ROWS):
                 source = (lane + row + start) % LANES
@@ -217,7 +239,7 @@
         out_shape=(jax.ShapeDtypeStruct((2, 1, ch, band), jnp.float32),)
         + (product_shape(ch),) * len(keep),
         scratch_shapes=[
-            pltpu.VMEM((depth, ch), jnp.bfloat16),
+            pltpu.VMEM((count, depth, ch), jnp.bfloat16),
             pltpu.VMEM((count,) + product_shape(ch).shape, jnp.float32),
             pltpu.VMEM((2, ch, (count - 1) * ch), jnp.float32),
             pltpu.SemaphoreType.DMA((2, 2)),
@@ -234,9 +256,10 @@
     _, pieces, lanes = own.shape
     band = (len(blocks) - 1) * pieces * lanes // 2
     left, own_product = own_terms(own)
-    out, third_product = region(left, [third, fourth], 3, band, keep=(0,))
-    out, second_product = region(left, [second, third_product], 2, band, out, keep=(0,))
-    out, = region(left, [own_product, first, second_product], 0, band, out)
+    fourth_product = block_product(left, fourth)
+    out, first_product = region(left, [own_product, first], 0, band, keep=(1,))
+    out, second_product = region(left, [first_product, second], 1, band, out, keep=(1,))
+    out, = region(left, [second_product, third, fourth_product], 2, band, out)
     return out
 
 
@@ -247,13 +270,15 @@
     def moved(array, pairs):
         return lax.ppermute(array, "chan", pairs)
 
-    fourth, third, second = (
-        moved(own, [(c, c - by) for c in range(by, count)]) for by in (half, 3, 2)
+    fourth = moved(own, [(c, c - half) for c in range(half, count)])
+    first = moved(own, [(c, c - 1) for c in range(1, count)])
+    handed = jnp.where(lax.axis_index("chan") < 2, fourth, own)
+    second = moved(
+        handed,
+        [(c, c - 2) for c in range(2, count) if c // half == (c - 2) // half]
+        + [(c, c + 2) for c in range(2)],
     )
-    handed = jnp.where(lax.axis_index("chan") == 0, fourth, own)
-    first = moved(
-        handed, [(c, c - 1) for c in range(1, count) if c != half] + [(0, half - 1)]
-    )
+    third = moved(handed, [(c, c - 3) for c in range(3, count)])
     return [first, second, third, fourth]
 
 

time: 51.8 us -> 54 us (1.042)
  the two profiles are of different devices: /device:TPU:6 before, /device:TPU:8 now
where the time goes in v5:
time: 54 us; the launch traced here: 53.8 us
  blocking collectives  29 us (54%)
  starting transfers between devices  8.8 us (16%)
  Pallas kernels  8.05 us (15%)
  waiting for transfers between devices  7.88 us (15%)
    all_to_all x1, blocking collectives, shards(): own = lax.all_to_all(bins, 'freq', split_axis=0, concat_axis=0, tiled=True)  29 us
    ppermute x4, starting transfers between devices, moved(): return lax.ppermute(array, 'chan', pairs)  8.8 us
    ppermute x4, waiting for transfers between devices, moved(): return lax.ppermute(array, 'chan', pairs)  7.88 us
    pallas_call x3, Pallas kernels, region(): pl.pallas_call(functools.partial(region_kernel, first, given, keep, fresh...  4.59 us
    pallas_call x1, Pallas kernels, whitened_bins(): pl.pallas_call(functools.partial(whiten_kernel, samples), in_specs=[pl.Bl...  2.65 us
  transfers between devices with their start and end apart: 4, of which 2 were waited for; matrix products, arithmetic and copies ran while one was open for 0% of the time, Pallas kernels for 7%

profile of v5, /device:TPU:8, one launch (start us, length us, event | category | flops | bytes accessed | tf_op | source)
XLA Modules:
  0.0 53.8 jit_solution(9144047122451805307)
XLA Ops:
  0.0 2.6 %whiten.1 = f32[64,4,128]{2,1,0:T(4,128)S(1)} custom-call(bf16[1,6144,256]{2,1,0:T(8,128)(2,1)} %record_ref.1), custom_call_target="tpu_custom_call" | custom-call | tf_op jit(solution)/shard_map/whiten/pallas_call | solution.py:86
  2.7 29.0 %all_to_all.5.own_ref = f32[64,4,128]{2,1,0:T(4,128)S(1)} all-to-all(f32[64,4,128]{2,1,0:T(4,128)S(1)} %whiten.1), channel_id=1, replica_groups=mesh['freq'=64,'chan'=8] {'freq'}, dimensions={0} | all-to-all | bytes 262144 | tf_op jit(solution)/shard_map/all_to_all | solution.py:287
  31.6 1.3 %collective-permute-start.1 = (f32[64,4,128]{2,1,0:T(4,128)S(1)}, f32[64,4,128]{2,1,0:T(4,128)S(1)}, u32[]{:S(2)}, u32[]{:S(2)}) collective-permute-start(f32[64,4,128]{2,1,0:T(4,128)S(1)} %all_to_all.5.own_ref), channel_id=1, source_target_pairs={{4,0},{5,1},{6,2},{7,3},{12,8},{13,9},{14,10},{15,11},{20,16},{21,... | collective-permute-start | bytes 393224 | tf_op jit(solution)/shard_map/ppermute | solution.py:271
  32.9 1.3 %collective-permute-start = (f32[64,4,128]{2,1,0:T(4,128)S(1)}, f32[64,4,128]{2,1,0:T(4,128)S(1)}, u32[]{:S(2)}, u32[]{:S(2)}) collective-permute-start(f32[64,4,128]{2,1,0:T(4,128)S(1)} %all_to_all.5.own_ref), channel_id=1, source_target_pairs={{1,0},{2,1},{3,2},{4,3},{5,4},{6,5},{7,6},{9,8},{10,9},{11,10},{12... | collective-permute-start | bytes 393224 | tf_op jit(solution)/shard_map/ppermute | solution.py:271
  34.2 4.8 %collective-permute-done.1.block_ref = f32[64,4,128]{2,1,0:T(4,128)S(1)} collective-permute-done((f32[64,4,128]{2,1,0:T(4,128)S(1)}, f32[64,4,128]{2,1,0:T(4,128)S(1)}, u32[]{:S(2)}, u32[]{:S(2)}) %collective-permute-start.1) | collective-permute-done | bytes 131104 | tf_op jit(solution)/shard_map/ppermute | solution.py:271
  39.0 4.9 %collective-permute-start.2 = (f32[64,4,128]{2,1,0:T(4,128)S(1)}, f32[64,4,128]{2,1,0:T(4,128)S(1)}, u32[]{:S(2)}, u32[]{:S(2)}) collective-permute-start(f32[64,4,128]{2,1,0:T(4,128)S(1)} %bitcast.5), channel_id=1, source_target_pairs={{2,0},{3,1},{6,4},{7,5},{0,2},{1,3},{10,8},{11,9},{14,12},{15,13},... | collective-permute-start | bytes 393224 | tf_op jit(solution)/shard_map/ppermute | solution.py:271
  44.0 1.3 %collective-permute-start.3 = (f32[64,4,128]{2,1,0:T(4,128)S(1)}, f32[64,4,128]{2,1,0:T(4,128)S(1)}, u32[]{:S(2)}, u32[]{:S(2)}) collective-permute-start(f32[64,4,128]{2,1,0:T(4,128)S(1)} %bitcast.6), channel_id=1, source_target_pairs={{3,0},{4,1},{5,2},{6,3},{7,4},{11,8},{12,9},{13,10},{14,11},{15,12... | collective-permute-start | bytes 393224 | tf_op jit(solution)/shard_map/ppermute | solution.py:271
  45.3 0.5 own.1
  45.7 0.3 product.1.refs_2_
  46.1 0.0 collective-permute-done.refs_1_
  46.1 1.4 %region.3 = (f32[2,1,256,1024]{3,2,1,0:T(8,128)}, f32[2,2,128,256]{3,2,1,0:T(8,128)S(1)}) custom-call(bf16[512,384]{1,0:T(8,128)(2,1)S(1)} %get-tuple-element.11.left_ref, f32[2,2,128,256]{3,2,1,0:T(8,128)S(1)} %get-tuple-element.12.refs_0_, f32[64,4,128]{2,1,0:T(4,128)S(1)} %collective-permute-done.refs_1_), custom_call_target="tpu_custom_call" | custom-call | bytes 3145728 | tf_op jit(solution)/shard_map/region/pallas_call | solution.py:235
  47.5 0.0 collective-permute-done.2.refs_1_
  47.5 1.4 %region.4 = (f32[2,1,256,1024]{3,2,1,0:T(8,128)}, f32[2,2,128,256]{3,2,1,0:T(8,128)S(1)}) custom-call(bf16[512,384]{1,0:T(8,128)(2,1)S(1)} %get-tuple-element.11.left_ref, f32[2,2,128,256]{3,2,1,0:T(8,128)S(1)} %get-tuple-element.13.refs_0_, f32[64,4,128]{2,1,0:T(4,128)S(1)} %collective-permute-done.2.refs_1_, ...), custom_call_target="tpu_custom_call", output_to_operand_aliasing={{0}: (3, {})} | custom-call | bytes 3145728 | tf_op jit(solution)/shard_map/region/pallas_call | solution.py:235
  49.0 3.1 %collective-permute-done.3.refs_1_ = f32[64,4,128]{2,1,0:T(4,128)S(1)} collective-permute-done((f32[64,4,128]{2,1,0:T(4,128)S(1)}, f32[64,4,128]{2,1,0:T(4,128)S(1)}, u32[]{:S(2)}, u32[]{:S(2)}) %collective-permute-start.3) | collective-permute-done | bytes 131104 | tf_op jit(solution)/shard_map/ppermute | solution.py:271
  52.0 1.8 %region.5 = f32[2,1,256,1024]{3,2,1,0:T(8,128)} custom-call(bf16[512,384]{1,0:T(8,128)(2,1)S(1)} %get-tuple-element.11.left_ref, f32[2,2,128,256]{3,2,1,0:T(8,128)S(1)} %get-tuple-element.15.refs_0_, f32[64,4,128]{2,1,0:T(4,128)S(1)} %collective-permute-done.3.refs_1_, f32[2,2,128,256]{3,2,1,0:T(8,128)S(1)} %product.1.refs_2_, ...), custom_call_target="tpu_custom_call", output_to_operand_aliasing={{}: (4, {})} | custom-call | bytes 3145728 | tf_op jit(solution)/shard_map/region/pallas_call | solution.py:235
  (1 shorter events, 0.0 us)
Async XLA Ops:
  31.6 7.4 %collective-permute-start.1 = (f32[64,4,128]{2,1,0:T(4,128)S(1)}, f32[64,4,128]{2,1,0:T(4,128)S(1)}, u32[]{:S(2)}, u32[]{:S(2)}) collective-permute-start(f32[64,4,128]{2,1,0:T(4,128)S(1)} %all_to_all.5.own_ref), channel_id=1, source_target_pairs={{4,0},{5,1},{6,2},{7,3},{12,8},{13,9},{14,10},{15,11},{20,16},{21,... | collective-permute-start | bytes 393224 | tf_op jit(solution)/shard_map/ppermute | solution.py:271
  32.9 13.2 %collective-permute-start = (f32[64,4,128]{2,1,0:T(4,128)S(1)}, f32[64,4,128]{2,1,0:T(4,128)S(1)}, u32[]{:S(2)}, u32[]{:S(2)}) collective-permute-start(f32[64,4,128]{2,1,0:T(4,128)S(1)} %all_to_all.5.own_ref), channel_id=1, source_target_pairs={{1,0},{2,1},{3,2},{4,3},{5,4},{6,5},{7,6},{9,8},{10,9},{11,10},{12... | collective-permute-start | bytes 393224 | tf_op jit(solution)/shard_map/ppermute | solution.py:271
  39.0 8.5 %collective-permute-start.2 = (f32[64,4,128]{2,1,0:T(4,128)S(1)}, f32[64,4,128]{2,1,0:T(4,128)S(1)}, u32[]{:S(2)}, u32[]{:S(2)}) collective-permute-start(f32[64,4,128]{2,1,0:T(4,128)S(1)} %bitcast.5), channel_id=1, source_target_pairs={{2,0},{3,1},{6,4},{7,5},{0,2},{1,3},{10,8},{11,9},{14,12},{15,13},... | collective-permute-start | bytes 393224 | tf_op jit(solution)/shard_map/ppermute | solution.py:271
  44.0 8.1 %collective-permute-start.3 = (f32[64,4,128]{2,1,0:T(4,128)S(1)}, f32[64,4,128]{2,1,0:T(4,128)S(1)}, u32[]{:S(2)}, u32[]{:S(2)}) collective-permute-start(f32[64,4,128]{2,1,0:T(4,128)S(1)} %bitcast.6), channel_id=1, source_target_pairs={{3,0},{4,1},{5,2},{6,3},{7,4},{11,8},{12,9},{13,10},{14,11},{15,12... | collective-permute-start | bytes 393224 | tf_op jit(solution)/shard_map/ppermute | solution.py:271

commit v6 on v5

--- a/solution.py
+++ b/solution.py
@@ -263,29 +263,16 @@
     return out
 
 
-def upper_blocks(own):
+def upper_block(own, offset):
     count = lax.axis_size("chan")
-    half = count // 2
-
-    def moved(array, pairs):
-        return lax.ppermute(array, "chan", pairs)
-
-    fourth = moved(own, [(c, c - half) for c in range(half, count)])
-    first = moved(own, [(c, c - 1) for c in range(1, count)])
-    handed = jnp.where(lax.axis_index("chan") < 2, fourth, own)
-    second = moved(
-        handed,
-        [(c, c - 2) for c in range(2, count) if c // half == (c - 2) // half]
-        + [(c, c + 2) for c in range(2)],
-    )
-    third = moved(handed, [(c, c - 3) for c in range(3, count)])
-    return [first, second, third, fourth]
+    return lax.ppermute(own, "chan", [(c, c - offset) for c in range(offset, count)])
 
 
 def shards(record):
     bins = whitened_bins(record)
     own = lax.all_to_all(bins, "freq", split_axis=0, concat_axis=0, tiled=True)
-    return cross_all([own] + upper_blocks(own))
+    reach = lax.axis_size("chan") // 2
+    return cross_all([own] + [upper_block(own, offset) for offset in range(1, reach + 1)])
 
 
 def solution(mesh):

time: 54 us -> 51.2 us (0.948)
  the two profiles are of different devices: /device:TPU:8 before, /device:TPU:6 now
where the time goes in v6:
time: 51.2 us; the launch traced here: 50.4 us
  blocking collectives  29.8 us (58%)
  starting transfers between devices  8.96 us (18%)
  Pallas kernels  8.04 us (16%)
  waiting for transfers between devices  3.48 us (7%)
    all_to_all x1, blocking collectives, shards(): own = lax.all_to_all(bins, 'freq', split_axis=0, concat_axis=0, tiled=True)  29.8 us
    ppermute x4, starting transfers between devices, upper_block(): lax.ppermute(own, 'chan', [(c, c - offset) for c in range(offset, count)])  8.96 us
    pallas_call x3, Pallas kernels, region(): pl.pallas_call(functools.partial(region_kernel, first, given, keep, fresh...  4.59 us
    ppermute x4, waiting for transfers between devices, upper_block(): lax.ppermute(own, 'chan', [(c, c - offset) for c in range(offset, count)])  3.48 us
    pallas_call x1, Pallas kernels, whitened_bins(): pl.pallas_call(functools.partial(whiten_kernel, samples), in_specs=[pl.Bl...  2.65 us
  transfers between devices with their start and end apart: 4, of which 2 were waited for; matrix products, arithmetic and copies ran while one was open for 0% of the time, Pallas kernels for 7%

profile of v6, /device:TPU:6, one launch (start us, length us, event | category | flops | bytes accessed | tf_op | source)
XLA Modules:
  0.0 50.4 jit_solution(12611176737526815097)
XLA Ops:
  0.0 2.6 %whiten.1 = f32[64,4,128]{2,1,0:T(4,128)S(1)} custom-call(bf16[1,6144,256]{2,1,0:T(8,128)(2,1)} %record_ref.1), custom_call_target="tpu_custom_call" | custom-call | tf_op jit(solution)/shard_map/whiten/pallas_call | solution.py:86
  2.7 29.8 %all_to_all.5.own_ref = f32[64,4,128]{2,1,0:T(4,128)S(1)} all-to-all(f32[64,4,128]{2,1,0:T(4,128)S(1)} %whiten.1), channel_id=1, replica_groups=mesh['freq'=64,'chan'=8] {'freq'}, dimensions={0} | all-to-all | bytes 262144 | tf_op jit(solution)/shard_map/all_to_all | solution.py:273
  32.5 1.3 %collective-permute-start.3 = (f32[64,4,128]{2,1,0:T(4,128)S(1)}, f32[64,4,128]{2,1,0:T(4,128)S(1)}, u32[]{:S(2)}, u32[]{:S(2)}) collective-permute-start(f32[64,4,128]{2,1,0:T(4,128)S(1)} %all_to_all.5.own_ref), channel_id=1, source_target_pairs={{4,0},{5,1},{6,2},{7,3},{12,8},{13,9},{14,10},{15,11},{20,16},{21,... | collective-permute-start | bytes 393224 | tf_op jit(solution)/shard_map/ppermute | solution.py:268
  33.8 2.7 %collective-permute-start = (f32[64,4,128]{2,1,0:T(4,128)S(1)}, f32[64,4,128]{2,1,0:T(4,128)S(1)}, u32[]{:S(2)}, u32[]{:S(2)}) collective-permute-start(f32[64,4,128]{2,1,0:T(4,128)S(1)} %all_to_all.5.own_ref), channel_id=1, source_target_pairs={{1,0},{2,1},{3,2},{4,3},{5,4},{6,5},{7,6},{9,8},{10,9},{11,10},{12... | collective-permute-start | bytes 393224 | tf_op jit(solution)/shard_map/ppermute | solution.py:268
  36.5 3.0 %collective-permute-start.1 = (f32[64,4,128]{2,1,0:T(4,128)S(1)}, f32[64,4,128]{2,1,0:T(4,128)S(1)}, u32[]{:S(2)}, u32[]{:S(2)}) collective-permute-start(f32[64,4,128]{2,1,0:T(4,128)S(1)} %all_to_all.5.own_ref), channel_id=1, source_target_pairs={{2,0},{3,1},{4,2},{5,3},{6,4},{7,5},{10,8},{11,9},{12,10},{13,11},... | collective-permute-start | bytes 393224 | tf_op jit(solution)/shard_map/ppermute | solution.py:268
  39.6 1.9 %collective-permute-start.2 = (f32[64,4,128]{2,1,0:T(4,128)S(1)}, f32[64,4,128]{2,1,0:T(4,128)S(1)}, u32[]{:S(2)}, u32[]{:S(2)}) collective-permute-start(f32[64,4,128]{2,1,0:T(4,128)S(1)} %all_to_all.5.own_ref), channel_id=1, source_target_pairs={{3,0},{4,1},{5,2},{6,3},{7,4},{11,8},{12,9},{13,10},{14,11},{15,12... | collective-permute-start | bytes 393224 | tf_op jit(solution)/shard_map/ppermute | solution.py:268
  41.5 0.5 own.1
  41.9 0.0 collective-permute-done.3.block_ref
  42.0 0.3 product.1.refs_2_
  42.3 1.5 %collective-permute-done.refs_1_ = f32[64,4,128]{2,1,0:T(4,128)S(1)} collective-permute-done((f32[64,4,128]{2,1,0:T(4,128)S(1)}, f32[64,4,128]{2,1,0:T(4,128)S(1)}, u32[]{:S(2)}, u32[]{:S(2)}) %collective-permute-start) | collective-permute-done | bytes 131104 | tf_op jit(solution)/shard_map/ppermute | solution.py:268
  43.8 1.4 %region.3 = (f32[2,1,256,1024]{3,2,1,0:T(8,128)}, f32[2,2,128,256]{3,2,1,0:T(8,128)S(1)}) custom-call(bf16[512,384]{1,0:T(8,128)(2,1)S(1)} %get-tuple-element.11.left_ref, f32[2,2,128,256]{3,2,1,0:T(8,128)S(1)} %get-tuple-element.12.refs_0_, f32[64,4,128]{2,1,0:T(4,128)S(1)} %collective-permute-done.refs_1_), custom_call_target="tpu_custom_call" | custom-call | bytes 3145728 | tf_op jit(solution)/shard_map/region/pallas_call | solution.py:235
  45.2 2.0 %collective-permute-done.1.refs_1_ = f32[64,4,128]{2,1,0:T(4,128)S(1)} collective-permute-done((f32[64,4,128]{2,1,0:T(4,128)S(1)}, f32[64,4,128]{2,1,0:T(4,128)S(1)}, u32[]{:S(2)}, u32[]{:S(2)}) %collective-permute-start.1) | collective-permute-done | bytes 131104 | tf_op jit(solution)/shard_map/ppermute | solution.py:268
  47.2 1.4 %region.4 = (f32[2,1,256,1024]{3,2,1,0:T(8,128)}, f32[2,2,128,256]{3,2,1,0:T(8,128)S(1)}) custom-call(bf16[512,384]{1,0:T(8,128)(2,1)S(1)} %get-tuple-element.11.left_ref, f32[2,2,128,256]{3,2,1,0:T(8,128)S(1)} %get-tuple-element.13.refs_0_, f32[64,4,128]{2,1,0:T(4,128)S(1)} %collective-permute-done.1.refs_1_, ...), custom_call_target="tpu_custom_call", output_to_operand_aliasing={{0}: (3, {})} | custom-call | bytes 3145728 | tf_op jit(solution)/shard_map/region/pallas_call | solution.py:235
  48.6 0.0 collective-permute-done.2.refs_1_
  48.6 1.8 %region.5 = f32[2,1,256,1024]{3,2,1,0:T(8,128)} custom-call(bf16[512,384]{1,0:T(8,128)(2,1)S(1)} %get-tuple-element.11.left_ref, f32[2,2,128,256]{3,2,1,0:T(8,128)S(1)} %get-tuple-element.15.refs_0_, f32[64,4,128]{2,1,0:T(4,128)S(1)} %collective-permute-done.2.refs_1_, f32[2,2,128,256]{3,2,1,0:T(8,128)S(1)} %product.1.refs_2_, ...), custom_call_target="tpu_custom_call", output_to_operand_aliasing={{}: (4, {})} | custom-call | bytes 3145728 | tf_op jit(solution)/shard_map/region/pallas_call | solution.py:235
Async XLA Ops:
  32.5 9.5 %collective-permute-start.3 = (f32[64,4,128]{2,1,0:T(4,128)S(1)}, f32[64,4,128]{2,1,0:T(4,128)S(1)}, u32[]{:S(2)}, u32[]{:S(2)}) collective-permute-start(f32[64,4,128]{2,1,0:T(4,128)S(1)} %all_to_all.5.own_ref), channel_id=1, source_target_pairs={{4,0},{5,1},{6,2},{7,3},{12,8},{13,9},{14,10},{15,11},{20,16},{21,... | collective-permute-start | bytes 393224 | tf_op jit(solution)/shard_map/ppermute | solution.py:268
  33.8 10.0 %collective-permute-start = (f32[64,4,128]{2,1,0:T(4,128)S(1)}, f32[64,4,128]{2,1,0:T(4,128)S(1)}, u32[]{:S(2)}, u32[]{:S(2)}) collective-permute-start(f32[64,4,128]{2,1,0:T(4,128)S(1)} %all_to_all.5.own_ref), channel_id=1, source_target_pairs={{1,0},{2,1},{3,2},{4,3},{5,4},{6,5},{7,6},{9,8},{10,9},{11,10},{12... | collective-permute-start | bytes 393224 | tf_op jit(solution)/shard_map/ppermute | solution.py:268
  36.5 10.7 %collective-permute-start.1 = (f32[64,4,128]{2,1,0:T(4,128)S(1)}, f32[64,4,128]{2,1,0:T(4,128)S(1)}, u32[]{:S(2)}, u32[]{:S(2)}) collective-permute-start(f32[64,4,128]{2,1,0:T(4,128)S(1)} %all_to_all.5.own_ref), channel_id=1, source_target_pairs={{2,0},{3,1},{4,2},{5,3},{6,4},{7,5},{10,8},{11,9},{12,10},{13,11},... | collective-permute-start | bytes 393224 | tf_op jit(solution)/shard_map/ppermute | solution.py:268
  39.6 9.1 %collective-permute-start.2 = (f32[64,4,128]{2,1,0:T(4,128)S(1)}, f32[64,4,128]{2,1,0:T(4,128)S(1)}, u32[]{:S(2)}, u32[]{:S(2)}) collective-permute-start(f32[64,4,128]{2,1,0:T(4,128)S(1)} %all_to_all.5.own_ref), channel_id=1, source_target_pairs={{3,0},{4,1},{5,2},{6,3},{7,4},{11,8},{12,9},{13,10},{14,11},{15,12... | collective-permute-start | bytes 393224 | tf_op jit(solution)/shard_map/ppermute | solution.py:268

commit v7 on v6

--- a/solution.py
+++ b/solution.py
@@ -11,7 +11,7 @@
 NBIN = 64
 NEIGH = 40
 CHUNKS = 6
-ROWS = 64
+ROWS = 8
 LANES = 128
 
 
@@ -196,10 +196,10 @@
     for a in range(2):
         for n in fresh_blocks:
             product(left_ref, wide_ref.at[n], products[n], a)
-        for part in range(2):
-            for start in range(0, rows, ROWS):
-                source = (lane + row + start) % LANES
-                stays = lane < LANES - start - row
+        for start in range(0, rows, ROWS):
+            source = (lane + row + start) % LANES
+            stays = lane < LANES - start - row
+            for part in range(2):
 
                 def turned(tile):
                     n, lanes = divmod(tile, tiles)
@@ -213,6 +213,7 @@
                         jnp.where(stays, before, after)
                     )
                     before = after
+        for part in range(2):
             here = pl.ds(a * rows, rows)
             there = pl.ds(first * ch, (count - 1) * ch)
             copy = pltpu.make_async_copy(
@@ -258,8 +259,8 @@
     left, own_product = own_terms(own)
     fourth_product = block_product(left, fourth)
     out, first_product = region(left, [own_product, first], 0, band, keep=(1,))
-    out, second_product = region(left, [first_product, second], 1, band, out, keep=(1,))
-    out, = region(left, [second_product, third, fourth_product], 2, band, out)
+    second_product = block_product(left, second)
+    out, = region(left, [first_product, second_product, third, fourth_product], 1, band, out)
     return out
 
 

time: 51.2 us -> 51.5 us (level)
  waiting for transfers between devices: 3.48 us -> 5.31 us
  Pallas kernels: 8.04 us -> 7.17 us
  starting transfers between devices: 8.96 us -> 8.44 us
    ppermute x4, waiting for transfers between devices: 3.48 us -> 5.31 us  [upper_block(): lax.ppermute(own, 'chan', [(c, c - offset) for c in range(offset, count)])]
    pallas_call x3 -> x2, Pallas kernels: 4.59 us -> 3.37 us  [region(): pl.pallas_call(functools.partial(region_kernel, first, given, keep, fresh...]
    ppermute x4, starting transfers between devices: 8.96 us -> 8.44 us  [upper_block(): lax.ppermute(own, 'chan', [(c, c - offset) for c in range(offset, count)])]
  transfers between devices with their start and end apart: 4 -> 4, of which waited for: 2 -> 2; matrix products, arithmetic and copies ran while one was open for 0% -> 0% of each run, Pallas kernels for 7% -> 5%
where the time goes in v7:
time: 51.5 us; the launch traced here: 50.8 us
  blocking collectives  29.8 us (58%)
  starting transfers between devices  8.44 us (16%)
  Pallas kernels  7.17 us (14%)
  waiting for transfers between devices  5.31 us (10%)
    all_to_all x1, blocking collectives, shards(): own = lax.all_to_all(bins, 'freq', split_axis=0, concat_axis=0, tiled=True)  29.8 us
    ppermute x4, starting transfers between devices, upper_block(): lax.ppermute(own, 'chan', [(c, c - offset) for c in range(offset, count)])  8.44 us
    ppermute x4, waiting for transfers between devices, upper_block(): lax.ppermute(own, 'chan', [(c, c - offset) for c in range(offset, count)])  5.31 us
    pallas_call x2, Pallas kernels, region(): pl.pallas_call(functools.partial(region_kernel, first, given, keep, fresh...  3.37 us
    pallas_call x1, Pallas kernels, whitened_bins(): pl.pallas_call(functools.partial(whiten_kernel, samples), in_specs=[pl.Bl...  2.65 us
  transfers between devices with their start and end apart: 4, of which 2 were waited for; matrix products, arithmetic and copies ran while one was open for 0% of the time, Pallas kernels for 5%

profile of v7, /device:TPU:6, one launch (start us, length us, event | category | flops | bytes accessed | tf_op | source)
XLA Modules:
  0.0 50.8 jit_solution(5243632005254716614)
XLA Ops:
  0.0 2.6 %whiten.1 = f32[64,4,128]{2,1,0:T(4,128)S(1)} custom-call(bf16[1,6144,256]{2,1,0:T(8,128)(2,1)} %record_ref.1), custom_call_target="tpu_custom_call" | custom-call | tf_op jit(solution)/shard_map/whiten/pallas_call | solution.py:86
  2.7 29.8 %all_to_all.5.own_ref = f32[64,4,128]{2,1,0:T(4,128)S(1)} all-to-all(f32[64,4,128]{2,1,0:T(4,128)S(1)} %whiten.1), channel_id=1, replica_groups=mesh['freq'=64,'chan'=8] {'freq'}, dimensions={0} | all-to-all | bytes 262144 | tf_op jit(solution)/shard_map/all_to_all | solution.py:274
  32.5 1.3 %collective-permute-start.3 = (f32[64,4,128]{2,1,0:T(4,128)S(1)}, f32[64,4,128]{2,1,0:T(4,128)S(1)}, u32[]{:S(2)}, u32[]{:S(2)}) collective-permute-start(f32[64,4,128]{2,1,0:T(4,128)S(1)} %all_to_all.5.own_ref), channel_id=1, source_target_pairs={{4,0},{5,1},{6,2},{7,3},{12,8},{13,9},{14,10},{15,11},{20,16},{21,... | collective-permute-start | bytes 393224 | tf_op jit(solution)/shard_map/ppermute | solution.py:269
  33.8 3.3 %collective-permute-start.1 = (f32[64,4,128]{2,1,0:T(4,128)S(1)}, f32[64,4,128]{2,1,0:T(4,128)S(1)}, u32[]{:S(2)}, u32[]{:S(2)}) collective-permute-start(f32[64,4,128]{2,1,0:T(4,128)S(1)} %all_to_all.5.own_ref), channel_id=1, source_target_pairs={{2,0},{3,1},{4,2},{5,3},{6,4},{7,5},{10,8},{11,9},{12,10},{13,11},... | collective-permute-start | bytes 393224 | tf_op jit(solution)/shard_map/ppermute | solution.py:269
  37.1 1.9 %collective-permute-start = (f32[64,4,128]{2,1,0:T(4,128)S(1)}, f32[64,4,128]{2,1,0:T(4,128)S(1)}, u32[]{:S(2)}, u32[]{:S(2)}) collective-permute-start(f32[64,4,128]{2,1,0:T(4,128)S(1)} %all_to_all.5.own_ref), channel_id=1, source_target_pairs={{1,0},{2,1},{3,2},{4,3},{5,4},{6,5},{7,6},{9,8},{10,9},{11,10},{12... | collective-permute-start | bytes 393224 | tf_op jit(solution)/shard_map/ppermute | solution.py:269
  39.0 1.9 %collective-permute-start.2 = (f32[64,4,128]{2,1,0:T(4,128)S(1)}, f32[64,4,128]{2,1,0:T(4,128)S(1)}, u32[]{:S(2)}, u32[]{:S(2)}) collective-permute-start(f32[64,4,128]{2,1,0:T(4,128)S(1)} %all_to_all.5.own_ref), channel_id=1, source_target_pairs={{3,0},{4,1},{5,2},{6,3},{7,4},{11,8},{12,9},{13,10},{14,11},{15,12... | collective-permute-start | bytes 393224 | tf_op jit(solution)/shard_map/ppermute | solution.py:269
  41.0 0.5 own.1
  41.4 0.0 collective-permute-done.3.block_ref
  41.4 0.3 product.3.refs_3_
  41.8 2.0 %collective-permute-done.1.block_ref = f32[64,4,128]{2,1,0:T(4,128)S(1)} collective-permute-done((f32[64,4,128]{2,1,0:T(4,128)S(1)}, f32[64,4,128]{2,1,0:T(4,128)S(1)}, u32[]{:S(2)}, u32[]{:S(2)}) %collective-permute-start.1) | collective-permute-done | bytes 131104 | tf_op jit(solution)/shard_map/ppermute | solution.py:269
  43.8 0.3 product.2.refs_1_
  44.1 3.3 %collective-permute-done.refs_1_ = f32[64,4,128]{2,1,0:T(4,128)S(1)} collective-permute-done((f32[64,4,128]{2,1,0:T(4,128)S(1)}, f32[64,4,128]{2,1,0:T(4,128)S(1)}, u32[]{:S(2)}, u32[]{:S(2)}) %collective-permute-start) | collective-permute-done | bytes 131104 | tf_op jit(solution)/shard_map/ppermute | solution.py:269
  47.5 1.4 %region.2 = (f32[2,1,256,1024]{3,2,1,0:T(8,128)}, f32[2,2,128,256]{3,2,1,0:T(8,128)S(1)}) custom-call(bf16[512,384]{1,0:T(8,128)(2,1)S(1)} %get-tuple-element.9.left_ref, f32[2,2,128,256]{3,2,1,0:T(8,128)S(1)} %get-tuple-element.10.refs_0_, f32[64,4,128]{2,1,0:T(4,128)S(1)} %collective-permute-done.refs_1_), custom_call_target="tpu_custom_call" | custom-call | bytes 3145728 | tf_op jit(solution)/shard_map/region/pallas_call | solution.py:236
  48.9 0.0 collective-permute-done.2.refs_2_
  48.9 2.0 %region.3 = f32[2,1,256,1024]{3,2,1,0:T(8,128)} custom-call(bf16[512,384]{1,0:T(8,128)(2,1)S(1)} %get-tuple-element.9.left_ref, f32[2,2,128,256]{3,2,1,0:T(8,128)S(1)} %get-tuple-element.11.refs_0_, f32[2,2,128,256]{3,2,1,0:T(8,128)S(1)} %product.2.refs_1_, f32[64,4,128]{2,1,0:T(4,128)S(1)} %collective-permute-done.2.refs_2_, ...), custom_call_target="tpu_custom_call", output_to_operand_aliasing={{}: (5, {})} | custom-call | bytes 3145728 | tf_op jit(solution)/shard_map/region/pallas_call | solution.py:236
Async XLA Ops:
  32.5 8.9 %collective-permute-start.3 = (f32[64,4,128]{2,1,0:T(4,128)S(1)}, f32[64,4,128]{2,1,0:T(4,128)S(1)}, u32[]{:S(2)}, u32[]{:S(2)}) collective-permute-start(f32[64,4,128]{2,1,0:T(4,128)S(1)} %all_to_all.5.own_ref), channel_id=1, source_target_pairs={{4,0},{5,1},{6,2},{7,3},{12,8},{13,9},{14,10},{15,11},{20,16},{21,... | collective-permute-start | bytes 393224 | tf_op jit(solution)/shard_map/ppermute | solution.py:269
  33.8 10.0 %collective-permute-start.1 = (f32[64,4,128]{2,1,0:T(4,128)S(1)}, f32[64,4,128]{2,1,0:T(4,128)S(1)}, u32[]{:S(2)}, u32[]{:S(2)}) collective-permute-start(f32[64,4,128]{2,1,0:T(4,128)S(1)} %all_to_all.5.own_ref), channel_id=1, source_target_pairs={{2,0},{3,1},{4,2},{5,3},{6,4},{7,5},{10,8},{11,9},{12,10},{13,11},... | collective-permute-start | bytes 393224 | tf_op jit(solution)/shard_map/ppermute | solution.py:269
  37.1 10.4 %collective-permute-start = (f32[64,4,128]{2,1,0:T(4,128)S(1)}, f32[64,4,128]{2,1,0:T(4,128)S(1)}, u32[]{:S(2)}, u32[]{:S(2)}) collective-permute-start(f32[64,4,128]{2,1,0:T(4,128)S(1)} %all_to_all.5.own_ref), channel_id=1, source_target_pairs={{1,0},{2,1},{3,2},{4,3},{5,4},{6,5},{7,6},{9,8},{10,9},{11,10},{12... | collective-permute-start | bytes 393224 | tf_op jit(solution)/shard_map/ppermute | solution.py:269
  39.0 9.8 %collective-permute-start.2 = (f32[64,4,128]{2,1,0:T(4,128)S(1)}, f32[64,4,128]{2,1,0:T(4,128)S(1)}, u32[]{:S(2)}, u32[]{:S(2)}) collective-permute-start(f32[64,4,128]{2,1,0:T(4,128)S(1)} %all_to_all.5.own_ref), channel_id=1, source_target_pairs={{3,0},{4,1},{5,2},{6,3},{7,4},{11,8},{12,9},{13,10},{14,11},{15,12... | collective-permute-start | bytes 393224 | tf_op jit(solution)/shard_map/ppermute | solution.py:269

commit v8 on v7

--- a/solution.py
+++ b/solution.py
@@ -6,10 +6,11 @@
 from jax import lax
 from jax.experimental import pallas as pl
 from jax.experimental.pallas import tpu as pltpu
-from jax.sharding import PartitionSpec as P
+from jax.sharding import Mesh, PartitionSpec as P
 
 NBIN = 64
 NEIGH = 40
+GROUP = 8
 CHUNKS = 6
 ROWS = 8
 LANES = 128
@@ -20,9 +21,13 @@
     return high, (x - high.astype(jnp.float32)).astype(rest)
 
 
+def bin_of(row):
+    return (row & (GROUP - 1)) * GROUP + row // GROUP
+
+
 def smoothed(power):
-    row = lax.broadcasted_iota(jnp.int32, (NBIN, NBIN), 0)
-    col = lax.broadcasted_iota(jnp.int32, (NBIN, NBIN), 1)
+    row = bin_of(lax.broadcasted_iota(jnp.int32, (NBIN, NBIN), 0))
+    col = bin_of(lax.broadcasted_iota(jnp.int32, (NBIN, NBIN), 1))
     below, above = NEIGH // 2, NEIGH - NEIGH // 2
     inside = ((col - row >= -below) & (col - row < above)).astype(jnp.float32)
     inside = inside.astype(jnp.bfloat16)
@@ -33,14 +38,14 @@
         jnp.concatenate([high, middle, low], axis=0),
         preferred_element_type=jnp.float32,
     )
-    first = lax.broadcasted_iota(jnp.int32, power.shape, 0)
+    first = bin_of(lax.broadcasted_iota(jnp.int32, power.shape, 0))
     count = jnp.minimum(first + above, NBIN) - jnp.maximum(first - below, 0)
     return total / count.astype(jnp.float32)
 
 
 def base_angles(samples):
     stride, period = samples // (2 * NBIN), 2 * NBIN
-    k = lax.broadcasted_iota(jnp.int32, (NBIN, period), 0)
+    k = bin_of(lax.broadcasted_iota(jnp.int32, (NBIN, period), 0))
     s = lax.broadcasted_iota(jnp.int32, (NBIN, period), 1)
     phase = s + stride * ((k * s) & (period - 1))
     return 2.0 * math.pi / samples * phase.astype(jnp.float32)
@@ -118,7 +123,8 @@
     ).reshape(parts, rows, ch)
 
 
-def product_kernel(left_ref, block_ref, prod_ref, wide_ref):
+def product_kernel(left_ref, block_ref, *refs):
+    prod_ref, wide_ref = refs[-2:]
     spread(block_ref, wide_ref)
     for half in range(2):
         product(left_ref, wide_ref, prod_ref, half)
@@ -162,19 +168,19 @@
     )(own)
 
 
-def block_product(left, block):
+def block_product(left, block, *after):
     rows, depth = left.shape
     vmem = pl.BlockSpec(memory_space=pltpu.VMEM)
     return pl.pallas_call(
         product_kernel,
-        in_specs=[vmem, vmem],
+        in_specs=[vmem, vmem] + [pl.BlockSpec(memory_space=pl.ANY)] * len(after),
         out_specs=vmem,
         out_shape=product_shape(rows // 2),
         scratch_shapes=[pltpu.VMEM((depth, rows // 2), jnp.bfloat16)],
         compiler_params=pltpu.CompilerParams(vmem_limit_bytes=16 * 1024 * 1024),
         cost_estimate=pl.CostEstimate(flops=0, bytes_accessed=1 << 20, transcendentals=0),
         name="product",
-    )(left, block)
+    )(left, block, *after)
 
 
 def region_kernel(first, given, keep, fresh, left_ref, *refs):
@@ -259,7 +265,7 @@
     left, own_product = own_terms(own)
     fourth_product = block_product(left, fourth)
     out, first_product = region(left, [own_product, first], 0, band, keep=(1,))
-    second_product = block_product(left, second)
+    second_product = block_product(left, second, first_product)
     out, = region(left, [first_product, second_product, third, fourth_product], 1, band, out)
     return out
 
@@ -271,16 +277,17 @@
 
 def shards(record):
     bins = whitened_bins(record)
-    own = lax.all_to_all(bins, "freq", split_axis=0, concat_axis=0, tiled=True)
+    own = lax.all_to_all(bins, ("g", "y"), split_axis=0, concat_axis=0, tiled=True)
     reach = lax.axis_size("chan") // 2
     return cross_all([own] + [upper_block(own, offset) for offset in range(1, reach + 1)])
 
 
 def solution(mesh):
+    fine = Mesh(mesh.devices.reshape(GROUP, GROUP, -1), ("y", "g", "chan"))
     return jax.shard_map(
         shards,
-        mesh=mesh,
-        in_specs=(P("freq", None, "chan"),),
-        out_specs=P(None, "freq", "chan", None),
+        mesh=fine,
+        in_specs=(P(("y", "g"), None, "chan"),),
+        out_specs=P(None, ("y", "g"), "chan", None),
         check_vma=False,
     )

time: 51.5 us -> 50.8 us (0.986)
  the two profiles are of different devices: /device:TPU:6 before, /device:TPU:64 now
where the time goes in v8:
time: 50.8 us; the launch traced here: 50.5 us
  blocking collectives  28.9 us (57%)
  starting transfers between devices  10.6 us (21%)
  Pallas kernels  7.17 us (14%)
  waiting for transfers between devices  3.81 us (8%)
    all_to_all x1, blocking collectives, shards(): lax.all_to_all(bins, ('g', 'y'), split_axis=0, concat_axis=0, tiled=True)  28.9 us
    ppermute x4, starting transfers between devices, upper_block(): lax.ppermute(own, 'chan', [(c, c - offset) for c in range(offset, count)])  10.6 us
    ppermute x4, waiting for transfers between devices, upper_block(): lax.ppermute(own, 'chan', [(c, c - offset) for c in range(offset, count)])  3.81 us
    pallas_call x2, Pallas kernels, region(): pl.pallas_call(functools.partial(region_kernel, first, given, keep, fresh...  3.37 us
    pallas_call x1, Pallas kernels, whitened_bins(): pl.pallas_call(functools.partial(whiten_kernel, samples), in_specs=[pl.Bl...  2.65 us
  transfers between devices with their start and end apart: 4, of which 2 were waited for; matrix products, arithmetic and copies ran while one was open for 0% of the time, Pallas kernels for 5%

profile of v8, /device:TPU:64, one launch (start us, length us, event | category | flops | bytes accessed | tf_op | source)
XLA Modules:
  0.0 50.5 jit_solution(7958407200889026761)
XLA Ops:
  0.0 2.7 %whiten.1 = f32[64,4,128]{2,1,0:T(4,128)S(1)} custom-call(bf16[1,6144,256]{2,1,0:T(8,128)(2,1)} %record_ref.1), custom_call_target="tpu_custom_call" | custom-call | tf_op jit(solution)/shard_map/whiten/pallas_call | solution.py:91
  2.7 28.9 %all_to_all.5.own_ref = f32[64,4,128]{2,1,0:T(4,128)S(1)} all-to-all(f32[64,4,128]{2,1,0:T(4,128)S(1)} %whiten.1), channel_id=1, replica_groups=mesh['y'=8,'g'=8,'chan'=8] {'g','y'}, dimensions={0} | all-to-all | bytes 262144 | tf_op jit(solution)/shard_map/all_to_all | solution.py:280
  31.6 2.4 %collective-permute-start.3 = (f32[64,4,128]{2,1,0:T(4,128)S(1)}, f32[64,4,128]{2,1,0:T(4,128)S(1)}, u32[]{:S(2)}, u32[]{:S(2)}) collective-permute-start(f32[64,4,128]{2,1,0:T(4,128)S(1)} %all_to_all.5.own_ref), channel_id=1, source_target_pairs={{4,0},{5,1},{6,2},{7,3},{12,8},{13,9},{14,10},{15,11},{20,16},{21,... | collective-permute-start | bytes 393224 | tf_op jit(solution)/shard_map/ppermute | solution.py:275
  34.0 3.5 %collective-permute-start = (f32[64,4,128]{2,1,0:T(4,128)S(1)}, f32[64,4,128]{2,1,0:T(4,128)S(1)}, u32[]{:S(2)}, u32[]{:S(2)}) collective-permute-start(f32[64,4,128]{2,1,0:T(4,128)S(1)} %all_to_all.5.own_ref), channel_id=1, source_target_pairs={{1,0},{2,1},{3,2},{4,3},{5,4},{6,5},{7,6},{9,8},{10,9},{11,10},{12... | collective-permute-start | bytes 393224 | tf_op jit(solution)/shard_map/ppermute | solution.py:275
  37.5 2.7 %collective-permute-start.1 = (f32[64,4,128]{2,1,0:T(4,128)S(1)}, f32[64,4,128]{2,1,0:T(4,128)S(1)}, u32[]{:S(2)}, u32[]{:S(2)}) collective-permute-start(f32[64,4,128]{2,1,0:T(4,128)S(1)} %all_to_all.5.own_ref), channel_id=1, source_target_pairs={{2,0},{3,1},{4,2},{5,3},{6,4},{7,5},{10,8},{11,9},{12,10},{13,11},... | collective-permute-start | bytes 393224 | tf_op jit(solution)/shard_map/ppermute | solution.py:275
  40.2 1.9 %collective-permute-start.2 = (f32[64,4,128]{2,1,0:T(4,128)S(1)}, f32[64,4,128]{2,1,0:T(4,128)S(1)}, u32[]{:S(2)}, u32[]{:S(2)}) collective-permute-start(f32[64,4,128]{2,1,0:T(4,128)S(1)} %all_to_all.5.own_ref), channel_id=1, source_target_pairs={{3,0},{4,1},{5,2},{6,3},{7,4},{11,8},{12,9},{13,10},{14,11},{15,12... | collective-permute-start | bytes 393224 | tf_op jit(solution)/shard_map/ppermute | solution.py:275
  42.2 0.5 own.1
  42.6 0.0 collective-permute-done.3.block_ref
  42.6 0.3 product.3.refs_3_
  43.0 0.0 collective-permute-done.refs_1_
  43.0 1.4 %region.2 = (f32[2,1,256,1024]{3,2,1,0:T(8,128)}, f32[2,2,128,256]{3,2,1,0:T(8,128)S(1)}) custom-call(bf16[512,384]{1,0:T(8,128)(2,1)S(1)} %get-tuple-element.9.left_ref, f32[2,2,128,256]{3,2,1,0:T(8,128)S(1)} %get-tuple-element.10.refs_0_, f32[64,4,128]{2,1,0:T(4,128)S(1)} %collective-permute-done.refs_1_), custom_call_target="tpu_custom_call" | custom-call | bytes 3145728 | tf_op jit(solution)/shard_map/region/pallas_call | solution.py:242
  44.4 1.6 %collective-permute-done.1.block_ref = f32[64,4,128]{2,1,0:T(4,128)S(1)} collective-permute-done((f32[64,4,128]{2,1,0:T(4,128)S(1)}, f32[64,4,128]{2,1,0:T(4,128)S(1)}, u32[]{:S(2)}, u32[]{:S(2)}) %collective-permute-start.1) | collective-permute-done | bytes 131104 | tf_op jit(solution)/shard_map/ppermute | solution.py:275
  46.0 0.3 product.2.refs_1_
  46.3 2.2 %collective-permute-done.2.refs_2_ = f32[64,4,128]{2,1,0:T(4,128)S(1)} collective-permute-done((f32[64,4,128]{2,1,0:T(4,128)S(1)}, f32[64,4,128]{2,1,0:T(4,128)S(1)}, u32[]{:S(2)}, u32[]{:S(2)}) %collective-permute-start.2) | collective-permute-done | bytes 131104 | tf_op jit(solution)/shard_map/ppermute | solution.py:275
  48.6 2.0 %region.3 = f32[2,1,256,1024]{3,2,1,0:T(8,128)} custom-call(bf16[512,384]{1,0:T(8,128)(2,1)S(1)} %get-tuple-element.9.left_ref, f32[2,2,128,256]{3,2,1,0:T(8,128)S(1)} %get-tuple-element.11.refs_0_, f32[2,2,128,256]{3,2,1,0:T(8,128)S(1)} %product.2.refs_1_, f32[64,4,128]{2,1,0:T(4,128)S(1)} %collective-permute-done.2.refs_2_, ...), custom_call_target="tpu_custom_call", output_to_operand_aliasing={{}: (5, {})} | custom-call | bytes 3145728 | tf_op jit(solution)/shard_map/region/pallas_call | solution.py:242
Async XLA Ops:
  31.6 11.1 %collective-permute-start.3 = (f32[64,4,128]{2,1,0:T(4,128)S(1)}, f32[64,4,128]{2,1,0:T(4,128)S(1)}, u32[]{:S(2)}, u32[]{:S(2)}) collective-permute-start(f32[64,4,128]{2,1,0:T(4,128)S(1)} %all_to_all.5.own_ref), channel_id=1, source_target_pairs={{4,0},{5,1},{6,2},{7,3},{12,8},{13,9},{14,10},{15,11},{20,16},{21,... | collective-permute-start | bytes 393224 | tf_op jit(solution)/shard_map/ppermute | solution.py:275
  34.0 9.0 %collective-permute-start = (f32[64,4,128]{2,1,0:T(4,128)S(1)}, f32[64,4,128]{2,1,0:T(4,128)S(1)}, u32[]{:S(2)}, u32[]{:S(2)}) collective-permute-start(f32[64,4,128]{2,1,0:T(4,128)S(1)} %all_to_all.5.own_ref), channel_id=1, source_target_pairs={{1,0},{2,1},{3,2},{4,3},{5,4},{6,5},{7,6},{9,8},{10,9},{11,10},{12... | collective-permute-start | bytes 393224 | tf_op jit(solution)/shard_map/ppermute | solution.py:275
  37.5 8.5 %collective-permute-start.1 = (f32[64,4,128]{2,1,0:T(4,128)S(1)}, f32[64,4,128]{2,1,0:T(4,128)S(1)}, u32[]{:S(2)}, u32[]{:S(2)}) collective-permute-start(f32[64,4,128]{2,1,0:T(4,128)S(1)} %all_to_all.5.own_ref), channel_id=1, source_target_pairs={{2,0},{3,1},{4,2},{5,3},{6,4},{7,5},{10,8},{11,9},{12,10},{13,11},... | collective-permute-start | bytes 393224 | tf_op jit(solution)/shard_map/ppermute | solution.py:275
  40.2 8.3 %collective-permute-start.2 = (f32[64,4,128]{2,1,0:T(4,128)S(1)}, f32[64,4,128]{2,1,0:T(4,128)S(1)}, u32[]{:S(2)}, u32[]{:S(2)}) collective-permute-start(f32[64,4,128]{2,1,0:T(4,128)S(1)} %all_to_all.5.own_ref), channel_id=1, source_target_pairs={{3,0},{4,1},{5,2},{6,3},{7,4},{11,8},{12,9},{13,10},{14,11},{15,12... | collective-permute-start | bytes 393224 | tf_op jit(solution)/shard_map/ppermute | solution.py:275

commit v9 on v8

--- a/solution.py
+++ b/solution.py
@@ -6,11 +6,10 @@
 from jax import lax
 from jax.experimental import pallas as pl
 from jax.experimental.pallas import tpu as pltpu
-from jax.sharding import Mesh, PartitionSpec as P
+from jax.sharding import PartitionSpec as P
 
 NBIN = 64
 NEIGH = 40
-GROUP = 8
 CHUNKS = 6
 ROWS = 8
 LANES = 128
@@ -22,7 +21,7 @@
 
 
 def bin_of(row):
-    return (row & (GROUP - 1)) * GROUP + row // GROUP
+    return (row & 7) * 8 + (3 - (row >> 4)) * 2 + ((row >> 3) & 1)
 
 
 def smoothed(power):
@@ -277,17 +276,19 @@
 
 def shards(record):
     bins = whitened_bins(record)
-    own = lax.all_to_all(bins, ("g", "y"), split_axis=0, concat_axis=0, tiled=True)
+    own = lax.all_to_all(
+        bins, "freq", split_axis=0, concat_axis=0, tiled=True,
+        axis_index_groups=[[bin_of(row) for row in range(NBIN)]],
+    )
     reach = lax.axis_size("chan") // 2
     return cross_all([own] + [upper_block(own, offset) for offset in range(1, reach + 1)])
 
 
 def solution(mesh):
-    fine = Mesh(mesh.devices.reshape(GROUP, GROUP, -1), ("y", "g", "chan"))
     return jax.shard_map(
         shards,
-        mesh=fine,
-        in_specs=(P(("y", "g"), None, "chan"),),
-        out_specs=P(None, ("y", "g"), "chan", None),
+        mesh=mesh,
+        in_specs=(P("freq", None, "chan"),),
+        out_specs=P(None, "freq", "chan", None),
         check_vma=False,
     )

time: 50.8 us -> 47.7 us (0.939)
  blocking collectives: 28.9 us -> 25.8 us
    all_to_all x1, blocking collectives: 28.9 us -> 25.8 us  [shards(): lax.all_to_all(bins, 'freq', split_axis=0, concat_axis=0, tiled=True, axi...]
where the time goes in v9:
time: 47.7 us; the launch traced here: 47.4 us
  blocking collectives  25.8 us (54%)
  starting transfers between devices  10.6 us (22%)
  Pallas kernels  7.18 us (15%)
  waiting for transfers between devices  3.83 us (8%)
    all_to_all x1, blocking collectives, shards(): lax.all_to_all(bins, 'freq', split_axis=0, concat_axis=0, tiled=True, axi...  25.8 us
    ppermute x4, starting transfers between devices, upper_block(): lax.ppermute(own, 'chan', [(c, c - offset) for c in range(offset, count)])  10.6 us
    ppermute x4, waiting for transfers between devices, upper_block(): lax.ppermute(own, 'chan', [(c, c - offset) for c in range(offset, count)])  3.83 us
    pallas_call x2, Pallas kernels, region(): pl.pallas_call(functools.partial(region_kernel, first, given, keep, fresh...  3.37 us
    pallas_call x1, Pallas kernels, whitened_bins(): pl.pallas_call(functools.partial(whiten_kernel, samples), in_specs=[pl.Bl...  2.65 us
  transfers between devices with their start and end apart: 4, of which 2 were waited for; matrix products, arithmetic and copies ran while one was open for 0% of the time, Pallas kernels for 5%

profile of v9, /device:TPU:64, one launch (start us, length us, event | category | flops | bytes accessed | tf_op | source)
XLA Modules:
  0.0 47.4 jit_solution(8450499122528919134)
XLA Ops:
  0.0 2.7 %whiten.1 = f32[64,4,128]{2,1,0:T(4,128)S(1)} custom-call(bf16[1,6144,256]{2,1,0:T(8,128)(2,1)} %record_ref.1), custom_call_target="tpu_custom_call" | custom-call | tf_op jit(solution)/shard_map/whiten/pallas_call | solution.py:90
  2.7 25.8 %all_to_all.5.own_ref = f32[64,4,128]{2,1,0:T(4,128)S(1)} all-to-all(f32[64,4,128]{2,1,0:T(4,128)S(1)} %whiten.1), channel_id=1, replica_groups={{48,112,176,240,304,368,432,496,56,120,184,248,312,376,440,504,32,96,16..., dimensions={0} | all-to-all | bytes 262144 | tf_op jit(solution)/shard_map/all_to_all | solution.py:279
  28.4 2.4 %collective-permute-start.3 = (f32[64,4,128]{2,1,0:T(4,128)S(1)}, f32[64,4,128]{2,1,0:T(4,128)S(1)}, u32[]{:S(2)}, u32[]{:S(2)}) collective-permute-start(f32[64,4,128]{2,1,0:T(4,128)S(1)} %all_to_all.5.own_ref), channel_id=1, source_target_pairs={{4,0},{5,1},{6,2},{7,3},{12,8},{13,9},{14,10},{15,11},{20,16},{21,... | collective-permute-start | bytes 393224 | tf_op jit(solution)/shard_map/ppermute | solution.py:274
  30.9 3.5 %collective-permute-start = (f32[64,4,128]{2,1,0:T(4,128)S(1)}, f32[64,4,128]{2,1,0:T(4,128)S(1)}, u32[]{:S(2)}, u32[]{:S(2)}) collective-permute-start(f32[64,4,128]{2,1,0:T(4,128)S(1)} %all_to_all.5.own_ref), channel_id=1, source_target_pairs={{1,0},{2,1},{3,2},{4,3},{5,4},{6,5},{7,6},{9,8},{10,9},{11,10},{12... | collective-permute-start | bytes 393224 | tf_op jit(solution)/shard_map/ppermute | solution.py:274
  34.4 2.7 %collective-permute-start.1 = (f32[64,4,128]{2,1,0:T(4,128)S(1)}, f32[64,4,128]{2,1,0:T(4,128)S(1)}, u32[]{:S(2)}, u32[]{:S(2)}) collective-permute-start(f32[64,4,128]{2,1,0:T(4,128)S(1)} %all_to_all.5.own_ref), channel_id=1, source_target_pairs={{2,0},{3,1},{4,2},{5,3},{6,4},{7,5},{10,8},{11,9},{12,10},{13,11},... | collective-permute-start | bytes 393224 | tf_op jit(solution)/shard_map/ppermute | solution.py:274
  37.1 1.9 %collective-permute-start.2 = (f32[64,4,128]{2,1,0:T(4,128)S(1)}, f32[64,4,128]{2,1,0:T(4,128)S(1)}, u32[]{:S(2)}, u32[]{:S(2)}) collective-permute-start(f32[64,4,128]{2,1,0:T(4,128)S(1)} %all_to_all.5.own_ref), channel_id=1, source_target_pairs={{3,0},{4,1},{5,2},{6,3},{7,4},{11,8},{12,9},{13,10},{14,11},{15,12... | collective-permute-start | bytes 393224 | tf_op jit(solution)/shard_map/ppermute | solution.py:274
  39.0 0.5 own.1
  39.5 0.0 collective-permute-done.3.block_ref
  39.5 0.3 product.3.refs_3_
  39.9 0.0 collective-permute-done.refs_1_
  39.9 1.4 %region.2 = (f32[2,1,256,1024]{3,2,1,0:T(8,128)}, f32[2,2,128,256]{3,2,1,0:T(8,128)S(1)}) custom-call(bf16[512,384]{1,0:T(8,128)(2,1)S(1)} %get-tuple-element.9.left_ref, f32[2,2,128,256]{3,2,1,0:T(8,128)S(1)} %get-tuple-element.10.refs_0_, f32[64,4,128]{2,1,0:T(4,128)S(1)} %collective-permute-done.refs_1_), custom_call_target="tpu_custom_call" | custom-call | bytes 3145728 | tf_op jit(solution)/shard_map/region/pallas_call | solution.py:241
  41.3 1.6 %collective-permute-done.1.block_ref = f32[64,4,128]{2,1,0:T(4,128)S(1)} collective-permute-done((f32[64,4,128]{2,1,0:T(4,128)S(1)}, f32[64,4,128]{2,1,0:T(4,128)S(1)}, u32[]{:S(2)}, u32[]{:S(2)}) %collective-permute-start.1) | collective-permute-done | bytes 131104 | tf_op jit(solution)/shard_map/ppermute | solution.py:274
  42.9 0.3 product.2.refs_1_
  43.2 2.2 %collective-permute-done.2.refs_2_ = f32[64,4,128]{2,1,0:T(4,128)S(1)} collective-permute-done((f32[64,4,128]{2,1,0:T(4,128)S(1)}, f32[64,4,128]{2,1,0:T(4,128)S(1)}, u32[]{:S(2)}, u32[]{:S(2)}) %collective-permute-start.2) | collective-permute-done | bytes 131104 | tf_op jit(solution)/shard_map/ppermute | solution.py:274
  45.5 2.0 %region.3 = f32[2,1,256,1024]{3,2,1,0:T(8,128)} custom-call(bf16[512,384]{1,0:T(8,128)(2,1)S(1)} %get-tuple-element.9.left_ref, f32[2,2,128,256]{3,2,1,0:T(8,128)S(1)} %get-tuple-element.11.refs_0_, f32[2,2,128,256]{3,2,1,0:T(8,128)S(1)} %product.2.refs_1_, f32[64,4,128]{2,1,0:T(4,128)S(1)} %collective-permute-done.2.refs_2_, ...), custom_call_target="tpu_custom_call", output_to_operand_aliasing={{}: (5, {})} | custom-call | bytes 3145728 | tf_op jit(solution)/shard_map/region/pallas_call | solution.py:241
Async XLA Ops:
  28.4 11.1 %collective-permute-start.3 = (f32[64,4,128]{2,1,0:T(4,128)S(1)}, f32[64,4,128]{2,1,0:T(4,128)S(1)}, u32[]{:S(2)}, u32[]{:S(2)}) collective-permute-start(f32[64,4,128]{2,1,0:T(4,128)S(1)} %all_to_all.5.own_ref), channel_id=1, source_target_pairs={{4,0},{5,1},{6,2},{7,3},{12,8},{13,9},{14,10},{15,11},{20,16},{21,... | collective-permute-start | bytes 393224 | tf_op jit(solution)/shard_map/ppermute | solution.py:274
  30.9 9.0 %collective-permute-start = (f32[64,4,128]{2,1,0:T(4,128)S(1)}, f32[64,4,128]{2,1,0:T(4,128)S(1)}, u32[]{:S(2)}, u32[]{:S(2)}) collective-permute-start(f32[64,4,128]{2,1,0:T(4,128)S(1)} %all_to_all.5.own_ref), channel_id=1, source_target_pairs={{1,0},{2,1},{3,2},{4,3},{5,4},{6,5},{7,6},{9,8},{10,9},{11,10},{12... | collective-permute-start | bytes 393224 | tf_op jit(solution)/shard_map/ppermute | solution.py:274
  34.4 8.5 %collective-permute-start.1 = (f32[64,4,128]{2,1,0:T(4,128)S(1)}, f32[64,4,128]{2,1,0:T(4,128)S(1)}, u32[]{:S(2)}, u32[]{:S(2)}) collective-permute-start(f32[64,4,128]{2,1,0:T(4,128)S(1)} %all_to_all.5.own_ref), channel_id=1, source_target_pairs={{2,0},{3,1},{4,2},{5,3},{6,4},{7,5},{10,8},{11,9},{12,10},{13,11},... | collective-permute-start | bytes 393224 | tf_op jit(solution)/shard_map/ppermute | solution.py:274
  37.1 8.4 %collective-permute-start.2 = (f32[64,4,128]{2,1,0:T(4,128)S(1)}, f32[64,4,128]{2,1,0:T(4,128)S(1)}, u32[]{:S(2)}, u32[]{:S(2)}) collective-permute-start(f32[64,4,128]{2,1,0:T(4,128)S(1)} %all_to_all.5.own_ref), channel_id=1, source_target_pairs={{3,0},{4,1},{5,2},{6,3},{7,4},{11,8},{12,9},{13,10},{14,11},{15,12... | collective-permute-start | bytes 393224 | tf_op jit(solution)/shard_map/ppermute | solution.py:274

commit v10 on v9

--- a/solution.py
+++ b/solution.py
@@ -21,7 +21,9 @@
 
 
 def bin_of(row):
-    return (row & 7) * 8 + (3 - (row >> 4)) * 2 + ((row >> 3) & 1)
+    step = (row >> 1) & 3
+    y = 4 + step - (row & 1) * (1 + 2 * step)
+    return y * 8 + (3 - (row >> 4)) * 2 + ((row >> 3) & 1)
 
 
 def smoothed(power):

time: 47.7 us -> 44.9 us (0.941)
  blocking collectives: 25.8 us -> 22.9 us
    all_to_all x1, blocking collectives: 25.8 us -> 22.9 us  [shards(): lax.all_to_all(bins, 'freq', split_axis=0, concat_axis=0, tiled=True, axi...]
  transfers between devices with their start and end apart: 4 -> 4, of which waited for: 2 -> 2; matrix products, arithmetic and copies ran while one was open for 0% -> 0% of each run, Pallas kernels for 5% -> 6%
where the time goes in v10:
time: 44.9 us; the launch traced here: 44.7 us
  blocking collectives  22.9 us (51%)
  starting transfers between devices  10.6 us (24%)
  Pallas kernels  7.18 us (16%)
  waiting for transfers between devices  3.94 us (9%)
    all_to_all x1, blocking collectives, shards(): lax.all_to_all(bins, 'freq', split_axis=0, concat_axis=0, tiled=True, axi...  22.9 us
    ppermute x4, starting transfers between devices, upper_block(): lax.ppermute(own, 'chan', [(c, c - offset) for c in range(offset, count)])  10.6 us
    ppermute x4, waiting for transfers between devices, upper_block(): lax.ppermute(own, 'chan', [(c, c - offset) for c in range(offset, count)])  3.94 us
    pallas_call x2, Pallas kernels, region(): pl.pallas_call(functools.partial(region_kernel, first, given, keep, fresh...  3.37 us
    pallas_call x1, Pallas kernels, whitened_bins(): pl.pallas_call(functools.partial(whiten_kernel, samples), in_specs=[pl.Bl...  2.65 us
  transfers between devices with their start and end apart: 4, of which 2 were waited for; matrix products, arithmetic and copies ran while one was open for 0% of the time, Pallas kernels for 6%

profile of v10, /device:TPU:64, one launch (start us, length us, event | category | flops | bytes accessed | tf_op | source)
XLA Modules:
  0.0 44.7 jit_solution(1320532124727810603)
XLA Ops:
  0.0 2.7 %whiten.1 = f32[64,4,128]{2,1,0:T(4,128)S(1)} custom-call(bf16[1,6144,256]{2,1,0:T(8,128)(2,1)} %record_ref.1), custom_call_target="tpu_custom_call" | custom-call | tf_op jit(solution)/shard_map/whiten/pallas_call | solution.py:92
  2.7 22.9 %all_to_all.5.own_ref = f32[64,4,128]{2,1,0:T(4,128)S(1)} all-to-all(f32[64,4,128]{2,1,0:T(4,128)S(1)} %whiten.1), channel_id=1, replica_groups={{304,240,368,176,432,112,496,48,312,248,376,184,440,120,504,56,288,224,..., dimensions={0} | all-to-all | bytes 262144 | tf_op jit(solution)/shard_map/all_to_all | solution.py:281
  25.5 2.5 %collective-permute-start.3 = (f32[64,4,128]{2,1,0:T(4,128)S(1)}, f32[64,4,128]{2,1,0:T(4,128)S(1)}, u32[]{:S(2)}, u32[]{:S(2)}) collective-permute-start(f32[64,4,128]{2,1,0:T(4,128)S(1)} %all_to_all.5.own_ref), channel_id=1, source_target_pairs={{4,0},{5,1},{6,2},{7,3},{12,8},{13,9},{14,10},{15,11},{20,16},{21,... | collective-permute-start | bytes 393224 | tf_op jit(solution)/shard_map/ppermute | solution.py:276
  28.0 3.5 %collective-permute-start = (f32[64,4,128]{2,1,0:T(4,128)S(1)}, f32[64,4,128]{2,1,0:T(4,128)S(1)}, u32[]{:S(2)}, u32[]{:S(2)}) collective-permute-start(f32[64,4,128]{2,1,0:T(4,128)S(1)} %all_to_all.5.own_ref), channel_id=1, source_target_pairs={{1,0},{2,1},{3,2},{4,3},{5,4},{6,5},{7,6},{9,8},{10,9},{11,10},{12... | collective-permute-start | bytes 393224 | tf_op jit(solution)/shard_map/ppermute | solution.py:276
  31.5 2.7 %collective-permute-start.1 = (f32[64,4,128]{2,1,0:T(4,128)S(1)}, f32[64,4,128]{2,1,0:T(4,128)S(1)}, u32[]{:S(2)}, u32[]{:S(2)}) collective-permute-start(f32[64,4,128]{2,1,0:T(4,128)S(1)} %all_to_all.5.own_ref), channel_id=1, source_target_pairs={{2,0},{3,1},{4,2},{5,3},{6,4},{7,5},{10,8},{11,9},{12,10},{13,11},... | collective-permute-start | bytes 393224 | tf_op jit(solution)/shard_map/ppermute | solution.py:276
  34.2 1.9 %collective-permute-start.2 = (f32[64,4,128]{2,1,0:T(4,128)S(1)}, f32[64,4,128]{2,1,0:T(4,128)S(1)}, u32[]{:S(2)}, u32[]{:S(2)}) collective-permute-start(f32[64,4,128]{2,1,0:T(4,128)S(1)} %all_to_all.5.own_ref), channel_id=1, source_target_pairs={{3,0},{4,1},{5,2},{6,3},{7,4},{11,8},{12,9},{13,10},{14,11},{15,12... | collective-permute-start | bytes 393224 | tf_op jit(solution)/shard_map/ppermute | solution.py:276
  36.2 0.5 %own.1 = (bf16[512,384]{1,0:T(8,128)(2,1)S(1)}, f32[2,2,128,256]{3,2,1,0:T(8,128)S(1)}) custom-call(f32[64,4,128]{2,1,0:T(4,128)S(1)} %all_to_all.5.own_ref), custom_call_target="tpu_custom_call" | custom-call | bytes 1048576 | tf_op jit(solution)/shard_map/own/pallas_call | solution.py:157
  36.6 0.0 collective-permute-done.3.block_ref
  36.6 0.3 product.3.refs_3_
  37.0 0.0 collective-permute-done.refs_1_
  37.0 1.4 %region.2 = (f32[2,1,256,1024]{3,2,1,0:T(8,128)}, f32[2,2,128,256]{3,2,1,0:T(8,128)S(1)}) custom-call(bf16[512,384]{1,0:T(8,128)(2,1)S(1)} %get-tuple-element.9.left_ref, f32[2,2,128,256]{3,2,1,0:T(8,128)S(1)} %get-tuple-element.10.refs_0_, f32[64,4,128]{2,1,0:T(4,128)S(1)} %collective-permute-done.refs_1_), custom_call_target="tpu_custom_call" | custom-call | bytes 3145728 | tf_op jit(solution)/shard_map/region/pallas_call | solution.py:243
  38.4 1.6 %collective-permute-done.1.block_ref = f32[64,4,128]{2,1,0:T(4,128)S(1)} collective-permute-done((f32[64,4,128]{2,1,0:T(4,128)S(1)}, f32[64,4,128]{2,1,0:T(4,128)S(1)}, u32[]{:S(2)}, u32[]{:S(2)}) %collective-permute-start.1) | collective-permute-done | bytes 131104 | tf_op jit(solution)/shard_map/ppermute | solution.py:276
  40.0 0.3 product.2.refs_1_
  40.3 2.4 %collective-permute-done.2.refs_2_ = f32[64,4,128]{2,1,0:T(4,128)S(1)} collective-permute-done((f32[64,4,128]{2,1,0:T(4,128)S(1)}, f32[64,4,128]{2,1,0:T(4,128)S(1)}, u32[]{:S(2)}, u32[]{:S(2)}) %collective-permute-start.2) | collective-permute-done | bytes 131104 | tf_op jit(solution)/shard_map/ppermute | solution.py:276
  42.7 2.0 %region.3 = f32[2,1,256,1024]{3,2,1,0:T(8,128)} custom-call(bf16[512,384]{1,0:T(8,128)(2,1)S(1)} %get-tuple-element.9.left_ref, f32[2,2,128,256]{3,2,1,0:T(8,128)S(1)} %get-tuple-element.11.refs_0_, f32[2,2,128,256]{3,2,1,0:T(8,128)S(1)} %product.2.refs_1_, f32[64,4,128]{2,1,0:T(4,128)S(1)} %collective-permute-done.2.refs_2_, ...), custom_call_target="tpu_custom_call", output_to_operand_aliasing={{}: (5, {})} | custom-call | bytes 3145728 | tf_op jit(solution)/shard_map/region/pallas_call | solution.py:243
Async XLA Ops:
  25.5 11.1 %collective-permute-start.3 = (f32[64,4,128]{2,1,0:T(4,128)S(1)}, f32[64,4,128]{2,1,0:T(4,128)S(1)}, u32[]{:S(2)}, u32[]{:S(2)}) collective-permute-start(f32[64,4,128]{2,1,0:T(4,128)S(1)} %all_to_all.5.own_ref), channel_id=1, source_target_pairs={{4,0},{5,1},{6,2},{7,3},{12,8},{13,9},{14,10},{15,11},{20,16},{21,... | collective-permute-start | bytes 393224 | tf_op jit(solution)/shard_map/ppermute | solution.py:276
  28.0 9.0 %collective-permute-start = (f32[64,4,128]{2,1,0:T(4,128)S(1)}, f32[64,4,128]{2,1,0:T(4,128)S(1)}, u32[]{:S(2)}, u32[]{:S(2)}) collective-permute-start(f32[64,4,128]{2,1,0:T(4,128)S(1)} %all_to_all.5.own_ref), channel_id=1, source_target_pairs={{1,0},{2,1},{3,2},{4,3},{5,4},{6,5},{7,6},{9,8},{10,9},{11,10},{12... | collective-permute-start | bytes 393224 | tf_op jit(solution)/shard_map/ppermute | solution.py:276
  31.5 8.5 %collective-permute-start.1 = (f32[64,4,128]{2,1,0:T(4,128)S(1)}, f32[64,4,128]{2,1,0:T(4,128)S(1)}, u32[]{:S(2)}, u32[]{:S(2)}) collective-permute-start(f32[64,4,128]{2,1,0:T(4,128)S(1)} %all_to_all.5.own_ref), channel_id=1, source_target_pairs={{2,0},{3,1},{4,2},{5,3},{6,4},{7,5},{10,8},{11,9},{12,10},{13,11},... | collective-permute-start | bytes 393224 | tf_op jit(solution)/shard_map/ppermute | solution.py:276
  34.2 8.5 %collective-permute-start.2 = (f32[64,4,128]{2,1,0:T(4,128)S(1)}, f32[64,4,128]{2,1,0:T(4,128)S(1)}, u32[]{:S(2)}, u32[]{:S(2)}) collective-permute-start(f32[64,4,128]{2,1,0:T(4,128)S(1)} %all_to_all.5.own_ref), channel_id=1, source_target_pairs={{3,0},{4,1},{5,2},{6,3},{7,4},{11,8},{12,9},{13,10},{14,11},{15,12... | collective-permute-start | bytes 393224 | tf_op jit(solution)/shard_map/ppermute | solution.py:276

commit v11 on v9

--- a/solution.py
+++ b/solution.py
@@ -21,7 +21,9 @@
 
 
 def bin_of(row):
-    return (row & 7) * 8 + (3 - (row >> 4)) * 2 + ((row >> 3) & 1)
+    step = (row >> 2) & 3
+    y = 4 + step - ((row >> 1) & 1) * (1 + 2 * step)
+    return y * 8 + (3 - (row >> 4)) * 2 + (row & 1)
 
 
 def smoothed(power):

time: 47.7 us -> 45.1 us (0.945)
  the two profiles are of different devices: /device:TPU:64 before, /device:TPU:2 now
where the time goes in v11:
time: 45.1 us; the launch traced here: 44.9 us
  blocking collectives  23.7 us (53%)
  waiting for transfers between devices  7.62 us (17%)
  Pallas kernels  7.18 us (16%)
  starting transfers between devices  6.3 us (14%)
    all_to_all x1, blocking collectives, shards(): lax.all_to_all(bins, 'freq', split_axis=0, concat_axis=0, tiled=True, axi...  23.7 us
    ppermute x4, waiting for transfers between devices, upper_block(): lax.ppermute(own, 'chan', [(c, c - offset) for c in range(offset, count)])  7.62 us
    ppermute x4, starting transfers between devices, upper_block(): lax.ppermute(own, 'chan', [(c, c - offset) for c in range(offset, count)])  6.3 us
    pallas_call x2, Pallas kernels, region(): pl.pallas_call(functools.partial(region_kernel, first, given, keep, fresh...  3.37 us
    pallas_call x1, Pallas kernels, whitened_bins(): pl.pallas_call(functools.partial(whiten_kernel, samples), in_specs=[pl.Bl...  2.65 us
  transfers between devices with their start and end apart: 4, of which 4 were waited for; matrix products, arithmetic and copies ran while one was open for 0% of the time, Pallas kernels for 6%

profile of v11, /device:TPU:2, one launch (start us, length us, event | category | flops | bytes accessed | tf_op | source)
XLA Modules:
  0.0 44.9 jit_solution(6540196138945659403)
XLA Ops:
  0.0 2.7 %whiten.1 = f32[64,4,128]{2,1,0:T(4,128)S(1)} custom-call(bf16[1,6144,256]{2,1,0:T(8,128)(2,1)} %record_ref.1), custom_call_target="tpu_custom_call" | custom-call | tf_op jit(solution)/shard_map/whiten/pallas_call | solution.py:92
  2.7 23.7 %all_to_all.5.own_ref = f32[64,4,128]{2,1,0:T(4,128)S(1)} all-to-all(f32[64,4,128]{2,1,0:T(4,128)S(1)} %whiten.1), channel_id=1, replica_groups={{304,312,240,248,368,376,176,184,432,440,112,120,496,504,48,56,288,296,..., dimensions={0} | all-to-all | bytes 262144 | tf_op jit(solution)/shard_map/all_to_all | solution.py:281
  26.3 1.3 %collective-permute-start.3 = (f32[64,4,128]{2,1,0:T(4,128)S(1)}, f32[64,4,128]{2,1,0:T(4,128)S(1)}, u32[]{:S(2)}, u32[]{:S(2)}) collective-permute-start(f32[64,4,128]{2,1,0:T(4,128)S(1)} %all_to_all.5.own_ref), channel_id=1, source_target_pairs={{4,0},{5,1},{6,2},{7,3},{12,8},{13,9},{14,10},{15,11},{20,16},{21,... | collective-permute-start | bytes 393224 | tf_op jit(solution)/shard_map/ppermute | solution.py:276
  27.6 2.4 %collective-permute-start = (f32[64,4,128]{2,1,0:T(4,128)S(1)}, f32[64,4,128]{2,1,0:T(4,128)S(1)}, u32[]{:S(2)}, u32[]{:S(2)}) collective-permute-start(f32[64,4,128]{2,1,0:T(4,128)S(1)} %all_to_all.5.own_ref), channel_id=1, source_target_pairs={{1,0},{2,1},{3,2},{4,3},{5,4},{6,5},{7,6},{9,8},{10,9},{11,10},{12... | collective-permute-start | bytes 393224 | tf_op jit(solution)/shard_map/ppermute | solution.py:276
  30.1 1.3 %collective-permute-start.1 = (f32[64,4,128]{2,1,0:T(4,128)S(1)}, f32[64,4,128]{2,1,0:T(4,128)S(1)}, u32[]{:S(2)}, u32[]{:S(2)}) collective-permute-start(f32[64,4,128]{2,1,0:T(4,128)S(1)} %all_to_all.5.own_ref), channel_id=1, source_target_pairs={{2,0},{3,1},{4,2},{5,3},{6,4},{7,5},{10,8},{11,9},{12,10},{13,11},... | collective-permute-start | bytes 393224 | tf_op jit(solution)/shard_map/ppermute | solution.py:276
  31.4 1.3 %collective-permute-start.2 = (f32[64,4,128]{2,1,0:T(4,128)S(1)}, f32[64,4,128]{2,1,0:T(4,128)S(1)}, u32[]{:S(2)}, u32[]{:S(2)}) collective-permute-start(f32[64,4,128]{2,1,0:T(4,128)S(1)} %all_to_all.5.own_ref), channel_id=1, source_target_pairs={{3,0},{4,1},{5,2},{6,3},{7,4},{11,8},{12,9},{13,10},{14,11},{15,12... | collective-permute-start | bytes 393224 | tf_op jit(solution)/shard_map/ppermute | solution.py:276
  32.7 0.5 %own.1 = (bf16[512,384]{1,0:T(8,128)(2,1)S(1)}, f32[2,2,128,256]{3,2,1,0:T(8,128)S(1)}) custom-call(f32[64,4,128]{2,1,0:T(4,128)S(1)} %all_to_all.5.own_ref), custom_call_target="tpu_custom_call" | custom-call | bytes 1048576 | tf_op jit(solution)/shard_map/own/pallas_call | solution.py:157
  33.1 0.5 %collective-permute-done.3.block_ref = f32[64,4,128]{2,1,0:T(4,128)S(1)} collective-permute-done((f32[64,4,128]{2,1,0:T(4,128)S(1)}, f32[64,4,128]{2,1,0:T(4,128)S(1)}, u32[]{:S(2)}, u32[]{:S(2)}) %collective-permute-start.3) | collective-permute-done | bytes 131104 | tf_op jit(solution)/shard_map/ppermute | solution.py:276
  33.7 0.3 product.3.refs_3_
  34.0 0.9 %collective-permute-done.refs_1_ = f32[64,4,128]{2,1,0:T(4,128)S(1)} collective-permute-done((f32[64,4,128]{2,1,0:T(4,128)S(1)}, f32[64,4,128]{2,1,0:T(4,128)S(1)}, u32[]{:S(2)}, u32[]{:S(2)}) %collective-permute-start) | collective-permute-done | bytes 131104 | tf_op jit(solution)/shard_map/ppermute | solution.py:276
  35.0 1.4 %region.2 = (f32[2,1,256,1024]{3,2,1,0:T(8,128)}, f32[2,2,128,256]{3,2,1,0:T(8,128)S(1)}) custom-call(bf16[512,384]{1,0:T(8,128)(2,1)S(1)} %get-tuple-element.9.left_ref, f32[2,2,128,256]{3,2,1,0:T(8,128)S(1)} %get-tuple-element.10.refs_0_, f32[64,4,128]{2,1,0:T(4,128)S(1)} %collective-permute-done.refs_1_), custom_call_target="tpu_custom_call" | custom-call | bytes 3145728 | tf_op jit(solution)/shard_map/region/pallas_call | solution.py:243
  36.4 2.3 %collective-permute-done.1.block_ref = f32[64,4,128]{2,1,0:T(4,128)S(1)} collective-permute-done((f32[64,4,128]{2,1,0:T(4,128)S(1)}, f32[64,4,128]{2,1,0:T(4,128)S(1)}, u32[]{:S(2)}, u32[]{:S(2)}) %collective-permute-start.1) | collective-permute-done | bytes 131104 | tf_op jit(solution)/shard_map/ppermute | solution.py:276
  38.7 0.3 product.2.refs_1_
  39.1 3.8 %collective-permute-done.2.refs_2_ = f32[64,4,128]{2,1,0:T(4,128)S(1)} collective-permute-done((f32[64,4,128]{2,1,0:T(4,128)S(1)}, f32[64,4,128]{2,1,0:T(4,128)S(1)}, u32[]{:S(2)}, u32[]{:S(2)}) %collective-permute-start.2) | collective-permute-done | bytes 131104 | tf_op jit(solution)/shard_map/ppermute | solution.py:276
  42.9 2.0 %region.3 = f32[2,1,256,1024]{3,2,1,0:T(8,128)} custom-call(bf16[512,384]{1,0:T(8,128)(2,1)S(1)} %get-tuple-element.9.left_ref, f32[2,2,128,256]{3,2,1,0:T(8,128)S(1)} %get-tuple-element.11.refs_0_, f32[2,2,128,256]{3,2,1,0:T(8,128)S(1)} %product.2.refs_1_, f32[64,4,128]{2,1,0:T(4,128)S(1)} %collective-permute-done.2.refs_2_, ...), custom_call_target="tpu_custom_call", output_to_operand_aliasing={{}: (5, {})} | custom-call | bytes 3145728 | tf_op jit(solution)/shard_map/region/pallas_call | solution.py:243
Async XLA Ops:
  26.3 7.3 %collective-permute-start.3 = (f32[64,4,128]{2,1,0:T(4,128)S(1)}, f32[64,4,128]{2,1,0:T(4,128)S(1)}, u32[]{:S(2)}, u32[]{:S(2)}) collective-permute-start(f32[64,4,128]{2,1,0:T(4,128)S(1)} %all_to_all.5.own_ref), channel_id=1, source_target_pairs={{4,0},{5,1},{6,2},{7,3},{12,8},{13,9},{14,10},{15,11},{20,16},{21,... | collective-permute-start | bytes 393224 | tf_op jit(solution)/shard_map/ppermute | solution.py:276
  27.6 7.3 %collective-permute-start = (f32[64,4,128]{2,1,0:T(4,128)S(1)}, f32[64,4,128]{2,1,0:T(4,128)S(1)}, u32[]{:S(2)}, u32[]{:S(2)}) collective-permute-start(f32[64,4,128]{2,1,0:T(4,128)S(1)} %all_to_all.5.own_ref), channel_id=1, source_target_pairs={{1,0},{2,1},{3,2},{4,3},{5,4},{6,5},{7,6},{9,8},{10,9},{11,10},{12... | collective-permute-start | bytes 393224 | tf_op jit(solution)/shard_map/ppermute | solution.py:276
  30.1 8.6 %collective-permute-start.1 = (f32[64,4,128]{2,1,0:T(4,128)S(1)}, f32[64,4,128]{2,1,0:T(4,128)S(1)}, u32[]{:S(2)}, u32[]{:S(2)}) collective-permute-start(f32[64,4,128]{2,1,0:T(4,128)S(1)} %all_to_all.5.own_ref), channel_id=1, source_target_pairs={{2,0},{3,1},{4,2},{5,3},{6,4},{7,5},{10,8},{11,9},{12,10},{13,11},... | collective-permute-start | bytes 393224 | tf_op jit(solution)/shard_map/ppermute | solution.py:276
  31.4 11.5 %collective-permute-start.2 = (f32[64,4,128]{2,1,0:T(4,128)S(1)}, f32[64,4,128]{2,1,0:T(4,128)S(1)}, u32[]{:S(2)}, u32[]{:S(2)}) collective-permute-start(f32[64,4,128]{2,1,0:T(4,128)S(1)} %all_to_all.5.own_ref), channel_id=1, source_target_pairs={{3,0},{4,1},{5,2},{6,3},{7,4},{11,8},{12,9},{13,10},{14,11},{15,12... | collective-permute-start | bytes 393224 | tf_op jit(solution)/shard_map/ppermute | solution.py:276
